TPU v7x, 1024 devices: a whole 4x4x32 slice. The times are simulated.
1024 devices in a mesh: row: 128 (over y, z), col: 8 (over x, core).
Axes of the slice: x: 4, y: 4, z: 32, core: 2. Of those that a mesh axis runs over, the one named last changes fastest.
Arguments:
- right_side: float32 [128, 8, 8, 128], P('row', 'col'), may hold values from -6 to 6
- block_values: bfloat16 [128, 8, 8, 4, 128, 128], P('row', 'col'), may hold values from -0.25 to 0.25
- block_columns: int32 [128, 8, 8, 4], P('row', 'col'), may hold values from 0 to 71
- live_slots: int32 [128, 8, 8], P('row', 'col'), may hold values from 1 to 4
- row_scale: float32 [128, 8, 8, 128], P('row', 'col'), may hold values from 1 to 4
Outputs:
- solution_field: float32 [128, 8, 8, 128], P('row', 'col')
- hessenberg: float32 [5, 4], replicated
Inputs may be any that keep to these rules, and one draw needn't show every extreme that they name: `block_columns`: an entry q names block q % 8 of the device at grid offset (q // 24 - 1, (q // 8) % 3 - 1); blocks outside the grid are zero. Only the first live_slots slots of a block row are used.
All inputs are finite; a program needn't handle non-finite values.
Results may differ from a plain program's by a relative error of at most 0.0012.
Values may be sent and summed in bfloat16 or wider, within the bound.
No kernel may reach another device: no remote copies, remote signals or barrier semaphores. Data moves between devices by JAX's collectives and lax.ppermute only.
A program may use at most 32 MiB of HBM per device.

v0:
```python
import jax
import jax.numpy as jnp
from jax import lax
from jax.sharding import Mesh
from jax.sharding import PartitionSpec as P

ITERS = 4
ROW = ("row_0", "row_1")


def padded(x, sides, width):
    for axis, dim in sides:
        count, length = (lax.axis_size(axis), x.shape[dim])
        up = [(i, (i + 1) % count) for i in range(count - 1)]
        down = [(j, i) for i, j in up]
        last = lax.slice_in_dim(x, length - width, length, axis=dim)
        first = lax.slice_in_dim(x, 0, width, axis=dim)
        before = lax.ppermute(last, axis, up)
        after = lax.ppermute(first, axis, down)
        x = jnp.concatenate([before, x, after], axis=dim)
    return x


def sent_to_all(x, axis):
    copies = jnp.broadcast_to(x, (lax.axis_size(axis), *x.shape))
    return lax.all_to_all(copies, axis, split_axis=0, concat_axis=0, tiled=True)


def over_copies(x, axis):
    everything = sent_to_all(x, axis)
    return jnp.sum(everything, axis=0)


def together(arrays, axis):
    ends = [0]
    for a in arrays:
        ends.append(ends[-1] + a.size)
    total = over_copies(jnp.concatenate([a.ravel() for a in arrays]), axis)
    return tuple((total[b:e].reshape(a.shape) for a, b, e in zip(arrays, ends, ends[1:])))


def one_axis_at_a_time(x, axes):
    for axis in axes:
        x = lax.psum(x, axis)
    return x


def neighbourhood(rounded):
    return padded(rounded, ((ROW, 0), ("col", 1)), 1)


def global_sum(dot_terms, square_term):
    partial_dots, partial_square = together((dot_terms, square_term), "col")
    return (one_axis_at_a_time(partial_dots, ROW), one_axis_at_a_time(partial_square, ROW))


def least_squares(hessenberg, initial_norm):
    gram = jnp.dot(hessenberg.T, hessenberg, precision=lax.Precision.HIGHEST)
    target = initial_norm * hessenberg[0, :]
    factor = jnp.linalg.cholesky(gram)
    steps_count = gram.shape[0]
    forward = []
    for ordinal in range(steps_count):
        accum = target[ordinal]
        for other in range(ordinal):
            accum = accum - factor[ordinal, other] * forward[other]
        forward.append(accum / factor[ordinal, ordinal])
    backward = [None] * steps_count
    for ordinal in reversed(range(steps_count)):
        accum = forward[ordinal]
        for other in range(ordinal + 1, steps_count):
            accum = accum - factor[other, ordinal] * backward[other]
        backward[ordinal] = accum / factor[ordinal, ordinal]
    return backward


def on_device(right_side, block_values, block_columns, live_slots, row_scale):
    blocks_dev = right_side.shape[2]
    block_size = right_side.shape[3]
    slot_count = block_values.shape[3]
    values = block_values.reshape(blocks_dev, slot_count, block_size, block_size)
    slot_index = block_columns.reshape(-1)
    live_mask = (
        jnp.arange(slot_count, dtype=jnp.int32)[None, :] < live_slots.reshape(blocks_dev, 1)
    ).astype(jnp.bfloat16)[..., None]

    def operate(field):
        rounded = field.astype(jnp.bfloat16)
        beside_all = neighbourhood(rounded).reshape(9 * blocks_dev, block_size)
        picked = beside_all[slot_index].reshape(blocks_dev, slot_count, block_size) * live_mask
        product = jnp.einsum("nsij,nsj->ni", values, picked, preferred_element_type=jnp.float32)
        return row_scale * field + product.reshape(field.shape)

    first_image = operate(right_side)
    local_dots = jnp.stack([jnp.sum(right_side * right_side), jnp.sum(right_side * first_image)])
    summed_dots, image_dot = global_sum(local_dots, jnp.sum(first_image * first_image))
    self_dot = summed_dots[0]
    initial_norm = jnp.sqrt(self_dot)
    basis = [right_side / initial_norm]
    residue = first_image / initial_norm
    projections = jnp.stack([summed_dots[1] / self_dot])
    norm_square = image_dot / self_dot
    columns = []
    for iteration in range(ITERS):
        if iteration > 0:
            residue = operate(basis[-1])
            local_proj = jnp.stack([jnp.sum(vector * residue) for vector in basis])
            projections, norm_square = global_sum(local_proj, jnp.sum(residue * residue))
        height = jnp.sqrt(norm_square - jnp.sum(projections * projections))
        columns.append(
            jnp.concatenate(
                [projections, height[None], jnp.zeros((ITERS - iteration - 1,), jnp.float32)]
            )
        )
        if iteration + 1 < ITERS:
            for ordinal in range(len(basis)):
                residue = residue - projections[ordinal] * basis[ordinal]
            basis.append(residue / height)
    hessenberg = jnp.stack(columns, axis=1)
    weights = least_squares(hessenberg, initial_norm)
    solution_field = weights[0] * basis[0]
    for ordinal in range(1, ITERS):
        solution_field = solution_field + weights[ordinal] * basis[ordinal]
    return (solution_field, hessenberg)


def solution(mesh):
    finer = Mesh(mesh.devices.reshape(4, 32, mesh.shape["col"]), ("row_0", "row_1", "col"))
    in_specs = (
        P(ROW, "col", None, None),
        P(ROW, "col", None, None, None, None),
        P(ROW, "col", None, None),
        P(ROW, "col", None),
        P(ROW, "col", None, None),
    )
    out_specs = (P(ROW, "col", None, None), P())
    return jax.shard_map(
        on_device, mesh=finer, in_specs=in_specs, out_specs=out_specs, check_vma=False
    )
```

profile of v0, /device:TPU:32, one launch (start us, length us, event | category | flops | bytes accessed | tf_op | source)
XLA Modules:
  0.0 430.3 jit_solution(13028535033419592550)
XLA Ops:
  0.7 0.8 convert_element_type.19
  1.4 14.8 %collective-permute-start.1 = (bf16[1,1,8,128]{3,2,1,0:T(8,128)(2,1)S(1)}, bf16[1,1,8,128]{3,2,1,0:T(8,128)(2,1)S(1)}, u32[]{:S(2)}, u32[]{:S(2)}) collective-permute-start(bf16[1,1,8,128]{3,2,1,0:T(8,128)(2,1)S(1)} %convert_element_type.19), channel_id=1, source_target_pairs={{8,0},{16,8},{24,16},{32,24},{40,32},{48,40},{56,48},{64,56},{72,6... | collective-permute-start | bytes 6152 | tf_op jit(solution)/shard_map/ppermute | solution.py:19
  16.2 1.9 collective-permute-start
  18.4 3.3 collective-permute-done
  21.7 1.3 collective-permute-start.3
  23.0 3.0 collective-permute-start.2
  26.1 0.8 collective-permute-done.2
  26.9 0.6 gather_fusion
  28.2 0.7 multiply_reduce_fusion.14
  28.9 2.1 pad_maximum_fusion.9
  31.0 8.5 %all_to_all.24 = f32[8,1,3]{2,1,0:T(1,128)S(1)} all-to-all(f32[8,1,3]{2,1,0:T(1,128)S(1)} %broadcast_in_dim.30), channel_id=1, replica_groups=mesh['row_0'=4,'row_1'=32,'col'=8] {'col'}, dimensions={0} | all-to-all | bytes 192 | tf_op jit(solution)/shard_map/all_to_all | solution.py:26
  40.1 16.3 %all-reduce.7 = (f32[]{:T(128)}, f32[2]{0:T(128)S(1)}) all-reduce(f32[]{:T(128)} %bitcast.15, f32[2]{0:T(128)S(1)} %bitcast.128), channel_id=1, replica_groups=mesh['row_0'=4,'row_1'=32,'col'=8] {'row_0'}, use_global_device_ids=true, to_apply=%region_6.0 | all-reduce | flops 3 | bytes 24 | tf_op jit(solution)/shard_map/psum | solution.py:44
  56.3 57.5 %all-reduce.3 = (f32[]{:T(128)}, f32[2]{0:T(128)S(1)}) all-reduce(f32[]{:T(128)} %get-tuple-element.31, f32[2]{0:T(128)S(1)} %get-tuple-element.32), channel_id=1, replica_groups=mesh['row_0'=4,'row_1'=32,'col'=8] {'row_1'}, use_global_device_ids=true, to_apply=%region_7.0 | all-reduce | flops 3 | bytes 24 | tf_op jit(solution)/shard_map/psum | solution.py:44
  113.8 0.6 fusion.22
  117.9 1.9 collective-permute-start.5
  119.9 3.9 collective-permute-start.4
  123.8 1.6 collective-permute-done.4
  125.4 1.3 collective-permute-start.7
  126.7 3.0 collective-permute-start.6
  129.7 0.8 collective-permute-done.6
  130.5 0.6 gather_fusion.1
  131.6 0.7 multiply_reduce_fusion.11
  132.3 2.0 pad_maximum_fusion.10
  134.2 9.2 %all_to_all.25 = f32[8,1,3]{2,1,0:T(1,128)S(1)} all-to-all(f32[8,1,3]{2,1,0:T(1,128)S(1)} %broadcast_in_dim.32), channel_id=1, replica_groups=mesh['row_0'=4,'row_1'=32,'col'=8] {'col'}, dimensions={0} | all-to-all | bytes 192 | tf_op jit(solution)/shard_map/all_to_all | solution.py:26
  143.5 0.7 slice.115
  144.1 9.8 %all-reduce.6 = (f32[]{:T(128)}, f32[2]{0:T(128)S(1)}) all-reduce(f32[]{:T(128)} %bitcast.28, f32[2]{0:T(128)S(1)} %bitcast.129), channel_id=1, replica_groups=mesh['row_0'=4,'row_1'=32,'col'=8] {'row_0'}, use_global_device_ids=true, to_apply=%region_14.0 | all-reduce | flops 3 | bytes 24 | tf_op jit(solution)/shard_map/psum | solution.py:44
  153.9 57.4 %all-reduce.2 = (f32[]{:T(128)}, f32[2]{0:T(128)S(1)}) all-reduce(f32[]{:T(128)} %get-tuple-element.29, f32[2]{0:T(128)S(1)} %get-tuple-element.30), channel_id=1, replica_groups=mesh['row_0'=4,'row_1'=32,'col'=8] {'row_1'}, use_global_device_ids=true, to_apply=%region_15.0 | all-reduce | flops 3 | bytes 24 | tf_op jit(solution)/shard_map/psum | solution.py:44
  211.4 0.7 multiply_reduce_fusion.17
  212.0 0.6 fusion.21
  214.0 1.2 fusion.16
  215.2 1.9 collective-permute-start.9
  217.1 3.9 collective-permute-start.8
  221.1 1.6 collective-permute-done.8
  222.6 1.3 collective-permute-start.11
  223.9 3.0 collective-permute-start.10
  227.0 0.8 collective-permute-done.10
  227.8 0.6 gather_fusion.2
  228.8 0.7 multiply_reduce_fusion.8
  229.5 2.5 pad_maximum_fusion.11
  232.0 9.2 %all_to_all.26 = f32[8,1,4]{2,1,0:T(1,128)S(1)} all-to-all(f32[8,1,4]{2,1,0:T(1,128)S(1)} %broadcast_in_dim.34), channel_id=1, replica_groups=mesh['row_0'=4,'row_1'=32,'col'=8] {'col'}, dimensions={0} | all-to-all | bytes 256 | tf_op jit(solution)/shard_map/all_to_all | solution.py:26
  241.9 9.8 %all-reduce.5 = (f32[]{:T(128)}, f32[3]{0:T(128)S(1)}) all-reduce(f32[]{:T(128)} %bitcast.43, f32[3]{0:T(128)S(1)} %bitcast.130), channel_id=1, replica_groups=mesh['row_0'=4,'row_1'=32,'col'=8] {'row_0'}, use_global_device_ids=true, to_apply=%region_24.0 | all-reduce | flops 4 | bytes 32 | tf_op jit(solution)/shard_map/psum | solution.py:44
  251.7 57.3 %all-reduce.1 = (f32[]{:T(128)}, f32[3]{0:T(128)S(1)}) all-reduce(f32[]{:T(128)} %get-tuple-element.27, f32[3]{0:T(128)S(1)} %get-tuple-element.28), channel_id=1, replica_groups=mesh['row_0'=4,'row_1'=32,'col'=8] {'row_1'}, use_global_device_ids=true, to_apply=%region_25.0 | all-reduce | flops 4 | bytes 32 | tf_op jit(solution)/shard_map/psum | solution.py:44
  309.0 0.6 multiply_reduce_fusion.16
  309.6 0.6 fusion.20
  311.5 1.9 fusion.15
  313.4 1.9 collective-permute-start.13
  315.3 3.9 collective-permute-start.12
  319.3 1.5 collective-permute-done.12
  320.8 1.3 collective-permute-start.15
  322.1 3.0 collective-permute-start.14
  325.2 0.7 collective-permute-done.14
  327.0 0.7 multiply_reduce_fusion
  327.7 3.3 concatenate.62
  331.0 0.6 broadcast_in_dim.36
  331.6 4.2 all-to-all-start.3
  335.9 5.1 %all-to-all-done.3 = f32[8,1,5]{2,1,0:T(1,128)S(1)} async-done(((f32[8,1,5]{2,1,0:T(1,128)}), f32[8,1,5]{2,1,0:T(1,128)S(1)}, u32[]{:S(2)}, u32[]{:S(2)}) %all-to-all-start.3) | async-done | bytes 192 | tf_op jit(solution)/shard_map/all_to_all | solution.py:26
  341.6 9.8 %all-reduce.4 = (f32[]{:T(128)}, f32[4]{0:T(128)S(1)}) all-reduce(f32[]{:T(128)} %bitcast.60, f32[4]{0:T(128)S(1)} %bitcast.127), channel_id=1, replica_groups=mesh['row_0'=4,'row_1'=32,'col'=8] {'row_0'}, use_global_device_ids=true, to_apply=%region_35.0 | all-reduce | flops 5 | bytes 40 | tf_op jit(solution)/shard_map/psum | solution.py:44
  351.4 57.5 %all-reduce = (f32[]{:T(128)}, f32[4]{0:T(128)S(1)}) all-reduce(f32[]{:T(128)} %get-tuple-element.25, f32[4]{0:T(128)S(1)} %get-tuple-element.26), channel_id=1, replica_groups=mesh['row_0'=4,'row_1'=32,'col'=8] {'row_1'}, use_global_device_ids=true, to_apply=%region_36.0 | all-reduce | flops 5 | bytes 40 | tf_op jit(solution)/shard_map/psum | solution.py:44
  408.9 0.6 multiply_reduce_fusion.15
  412.0 0.6 compare_reduce_fusion
  412.6 0.6 select_select_fusion
  413.3 0.6 fusion.19
  413.9 0.7 fusion.18
  429.7 0.6 multiply_add_fusion
  (66 shorter events, 6.3 us)
Async XLA Ops:
  0.6 26.9 %copy-start = (bf16[1,1,8,4,128,128]{5,4,3,2,1,0:T(8,128)(2,1)S(1)}, bf16[1,1,8,4,128,128]{5,4,3,2,1,0:T(8,128)(2,1)}, u32[]{:S(2)}) copy-start(bf16[1,1,8,4,128,128]{5,4,3,2,1,0:T(8,128)(2,1)} %param.6) | copy-start | bytes 3145732
  0.6 17.5 %copy-start.5 = (s32[1,1,8]{2,1,0:T(1,128)S(1)}, s32[1,1,8]{2,1,0:T(1,128)}, u32[]{:S(2)}) copy-start(s32[1,1,8]{2,1,0:T(1,128)} %param.8) | copy-start | bytes 100
  1.4 16.8 %copy-start.4 = (s32[1,1,8,4]{2,3,1,0:T(4,128)S(1)}, s32[1,1,8,4]{2,3,1,0:T(4,128)}, u32[]{:S(2)}) copy-start(s32[1,1,8,4]{2,3,1,0:T(4,128)} %param.7) | copy-start | bytes 388
  1.4 17.0 %collective-permute-start.1 = (bf16[1,1,8,128]{3,2,1,0:T(8,128)(2,1)S(1)}, bf16[1,1,8,128]{3,2,1,0:T(8,128)(2,1)S(1)}, u32[]{:S(2)}, u32[]{:S(2)}) collective-permute-start(bf16[1,1,8,128]{3,2,1,0:T(8,128)(2,1)S(1)} %convert_element_type.19), channel_id=1, source_target_pairs={{8,0},{16,8},{24,16},{32,24},{40,32},{48,40},{56,48},{64,56},{72,6... | collective-permute-start | bytes 6152 | tf_op jit(solution)/shard_map/ppermute | solution.py:19
  16.2 5.5 %collective-permute-start = (bf16[1,1,8,128]{3,2,1,0:T(8,128)(2,1)S(1)}, bf16[1,1,8,128]{3,2,1,0:T(8,128)(2,1)S(1)}, u32[]{:S(2)}, u32[]{:S(2)}) collective-permute-start(bf16[1,1,8,128]{3,2,1,0:T(8,128)(2,1)S(1)} %convert_element_type.19), channel_id=1, source_target_pairs={{0,8},{8,16},{16,24},{24,32},{32,40},{40,48},{48,56},{56,64},{64,7... | collective-permute-start | bytes 6152 | tf_op jit(solution)/shard_map/ppermute | solution.py:18
  21.7 4.3 %collective-permute-start.3 = (bf16[3,1,8,128]{3,2,1,0:T(8,128)(2,1)S(1)}, bf16[3,1,8,128]{3,2,1,0:T(8,128)(2,1)S(1)}, u32[]{:S(2)}, u32[]{:S(2)}) collective-permute-start(bf16[3,1,8,128]{3,2,1,0:T(8,128)(2,1)S(1)} %pad_maximum_fusion.4), channel_id=1, source_target_pairs={{1,0},{2,1},{3,2},{4,3},{5,4},{6,5},{7,6},{9,8},{10,9},{11,10},{12... | collective-permute-start | bytes 18440 | tf_op jit(solution)/shard_map/ppermute | solution.py:19
  23.0 3.8 collective-permute-start.2
  27.5 0.7 copy-start.1
  27.6 0.7 copy-start.2
  117.9 5.9 %collective-permute-start.5 = (bf16[1,1,8,128]{3,2,1,0:T(8,128)(2,1)S(1)}, bf16[1,1,8,128]{3,2,1,0:T(8,128)(2,1)S(1)}, u32[]{:S(2)}, u32[]{:S(2)}) collective-permute-start(bf16[1,1,8,128]{3,2,1,0:T(8,128)(2,1)S(1)} %get-tuple-element.39), channel_id=1, source_target_pairs={{8,0},{16,8},{24,16},{32,24},{40,32},{48,40},{56,48},{64,56},{72,6... | collective-permute-start | bytes 6152 | tf_op jit(solution)/shard_map/ppermute | solution.py:19
  119.9 5.5 %collective-permute-start.4 = (bf16[1,1,8,128]{3,2,1,0:T(8,128)(2,1)S(1)}, bf16[1,1,8,128]{3,2,1,0:T(8,128)(2,1)S(1)}, u32[]{:S(2)}, u32[]{:S(2)}) collective-permute-start(bf16[1,1,8,128]{3,2,1,0:T(8,128)(2,1)S(1)} %get-tuple-element.39), channel_id=1, source_target_pairs={{0,8},{8,16},{16,24},{24,32},{32,40},{40,48},{48,56},{56,64},{64,7... | collective-permute-start | bytes 6152 | tf_op jit(solution)/shard_map/ppermute | solution.py:18
  125.4 4.3 %collective-permute-start.7 = (bf16[3,1,8,128]{3,2,1,0:T(8,128)(2,1)S(1)}, bf16[3,1,8,128]{3,2,1,0:T(8,128)(2,1)S(1)}, u32[]{:S(2)}, u32[]{:S(2)}) collective-permute-start(bf16[3,1,8,128]{3,2,1,0:T(8,128)(2,1)S(1)} %pad_maximum_fusion.5), channel_id=1, source_target_pairs={{1,0},{2,1},{3,2},{4,3},{5,4},{6,5},{7,6},{9,8},{10,9},{11,10},{12... | collective-permute-start | bytes 18440 | tf_op jit(solution)/shard_map/ppermute | solution.py:19
  126.7 3.8 collective-permute-start.6
  215.2 5.9 %collective-permute-start.9 = (bf16[1,1,8,128]{3,2,1,0:T(8,128)(2,1)S(1)}, bf16[1,1,8,128]{3,2,1,0:T(8,128)(2,1)S(1)}, u32[]{:S(2)}, u32[]{:S(2)}) collective-permute-start(bf16[1,1,8,128]{3,2,1,0:T(8,128)(2,1)S(1)} %get-tuple-element.36), channel_id=1, source_target_pairs={{8,0},{16,8},{24,16},{32,24},{40,32},{48,40},{56,48},{64,56},{72,6... | collective-permute-start | bytes 6152 | tf_op jit(solution)/shard_map/ppermute | solution.py:19
  217.1 5.5 %collective-permute-start.8 = (bf16[1,1,8,128]{3,2,1,0:T(8,128)(2,1)S(1)}, bf16[1,1,8,128]{3,2,1,0:T(8,128)(2,1)S(1)}, u32[]{:S(2)}, u32[]{:S(2)}) collective-permute-start(bf16[1,1,8,128]{3,2,1,0:T(8,128)(2,1)S(1)} %get-tuple-element.36), channel_id=1, source_target_pairs={{0,8},{8,16},{16,24},{24,32},{32,40},{40,48},{48,56},{56,64},{64,7... | collective-permute-start | bytes 6152 | tf_op jit(solution)/shard_map/ppermute | solution.py:18
  222.6 4.3 %collective-permute-start.11 = (bf16[3,1,8,128]{3,2,1,0:T(8,128)(2,1)S(1)}, bf16[3,1,8,128]{3,2,1,0:T(8,128)(2,1)S(1)}, u32[]{:S(2)}, u32[]{:S(2)}) collective-permute-start(bf16[3,1,8,128]{3,2,1,0:T(8,128)(2,1)S(1)} %pad_maximum_fusion.6), channel_id=1, source_target_pairs={{1,0},{2,1},{3,2},{4,3},{5,4},{6,5},{7,6},{9,8},{10,9},{11,10},{12... | collective-permute-start | bytes 18440 | tf_op jit(solution)/shard_map/ppermute | solution.py:19
  223.9 3.8 collective-permute-start.10
  313.4 5.9 %collective-permute-start.13 = (bf16[1,1,8,128]{3,2,1,0:T(8,128)(2,1)S(1)}, bf16[1,1,8,128]{3,2,1,0:T(8,128)(2,1)S(1)}, u32[]{:S(2)}, u32[]{:S(2)}) collective-permute-start(bf16[1,1,8,128]{3,2,1,0:T(8,128)(2,1)S(1)} %get-tuple-element.33), channel_id=1, source_target_pairs={{8,0},{16,8},{24,16},{32,24},{40,32},{48,40},{56,48},{64,56},{72,6... | collective-permute-start | bytes 6152 | tf_op jit(solution)/shard_map/ppermute | solution.py:19
  315.3 5.5 %collective-permute-start.12 = (bf16[1,1,8,128]{3,2,1,0:T(8,128)(2,1)S(1)}, bf16[1,1,8,128]{3,2,1,0:T(8,128)(2,1)S(1)}, u32[]{:S(2)}, u32[]{:S(2)}) collective-permute-start(bf16[1,1,8,128]{3,2,1,0:T(8,128)(2,1)S(1)} %get-tuple-element.33), channel_id=1, source_target_pairs={{0,8},{8,16},{16,24},{24,32},{32,40},{40,48},{48,56},{56,64},{64,7... | collective-permute-start | bytes 6152 | tf_op jit(solution)/shard_map/ppermute | solution.py:18
  320.8 4.4 %collective-permute-start.15 = (bf16[3,1,8,128]{3,2,1,0:T(8,128)(2,1)S(1)}, bf16[3,1,8,128]{3,2,1,0:T(8,128)(2,1)S(1)}, u32[]{:S(2)}, u32[]{:S(2)}) collective-permute-start(bf16[3,1,8,128]{3,2,1,0:T(8,128)(2,1)S(1)} %pad_maximum_fusion.7), channel_id=1, source_target_pairs={{1,0},{2,1},{3,2},{4,3},{5,4},{6,5},{7,6},{9,8},{10,9},{11,10},{12... | collective-permute-start | bytes 18440 | tf_op jit(solution)/shard_map/ppermute | solution.py:19
  322.1 3.8 collective-permute-start.14
  331.6 9.4 %all-to-all-start.3 = ((f32[8,1,5]{2,1,0:T(1,128)}), f32[8,1,5]{2,1,0:T(1,128)S(1)}, u32[]{:S(2)}, u32[]{:S(2)}) async-start(f32[8,1,5]{2,1,0:T(1,128)} %broadcast_in_dim.36), calls=%async_computation.3 | async-start | bytes 8192 | tf_op jit(solution)/shard_map/all_to_all | solution.py:26
  410.9 0.6 copy-start.3
where the time goes:
time: 432 us; the launch traced here: 430 us
  blocking collectives  302 us (70%)
  starting transfers between devices  55.7 us (13%)
  between operations  23.6 us (5%)
  other arithmetic  18.2 us (4%)
  waiting for transfers between devices  16.1 us (4%)
  local copies, waits for them, and re-layouts  12.9 us (3%)
    psum x8, blocking collectives, one_axis_at_a_time(): x = lax.psum(x, axis)  275 us
    all_to_all x3, blocking collectives, sent_to_all(): return lax.all_to_all(copies, axis, split_axis=0, concat_axis=0, tiled=True)  26.9 us
    ppermute x8, starting transfers between devices, padded(): before = lax.ppermute(last, axis, up)  25.8 us
    ppermute x8, starting transfers between devices, padded(): after = lax.ppermute(first, axis, down)  25.7 us
    ppermute x8, waiting for transfers between devices, padded(): before = lax.ppermute(last, axis, up)  11 us
  transfers between devices with their start and end apart: 17, of which 9 were waited for; matrix products, arithmetic and copies ran while one was open for 0% of the time, Pallas kernels for 0%

commit v1 on v0

v1 whole, which is shorter than its diff:
```python
import jax
import jax.numpy as jnp
from jax import lax
from jax.experimental import pallas as pl
from jax.experimental.pallas import tpu as pltpu
from jax.sharding import Mesh
from jax.sharding import PartitionSpec as P

ITERS = 4
NB = 8
BS = 128
SLOTS = 4
ROW = ("y", "z")
COL = ("x", "core")
PLANE = ("y", "x", "core")
SHIFT = 2.2
PAIRS = [(i, j) for j in range(ITERS + 1) for i in range(j + 1)]
F32 = jnp.float32
BF16 = jnp.bfloat16


def swaps(count):
    even = [(i, i ^ 1) for i in range(count)]
    odd = []
    for i in range(1, count - 1, 2):
        odd += [(i, i + 1), (i + 1, i)]
    return even, odd


def exchange(field, rows, cols):
    even, odd = swaps(rows)
    beside = jnp.stack(
        [field, lax.ppermute(field, ROW, even), lax.ppermute(field, ROW, odd)]
    )
    even, odd = swaps(cols)
    return (
        beside,
        lax.ppermute(beside, COL, even),
        lax.ppermute(beside, COL, odd),
    )


def fill(halo, parts):
    for at, part in enumerate(parts):
        for row in range(3):
            halo[pl.ds((at * 3 + row) * NB, NB), :] = part[row]
    halo[pl.ds(9 * NB, NB), :] = jnp.zeros((NB, BS), F32)


def multiply(index, halo, values, fine):
    sublane = lax.broadcasted_iota(jnp.int32, (NB, BS), 0)
    total = jnp.zeros((2 * NB, BS), F32)
    for n in range(NB):
        pieces = []
        for s in range(SLOTS):
            row = halo[pl.ds(index[n * SLOTS + s], 1), :]
            row = jnp.where(sublane == n, jnp.broadcast_to(row, (NB, BS)), 0.0)
            high = row.astype(BF16).astype(F32)
            low = row - high if fine else jnp.zeros_like(row)
            pieces.append(jnp.concatenate([high, low], axis=0).astype(BF16))
        left = jnp.concatenate(pieces, axis=1)
        right = jnp.concatenate([values[n * SLOTS + s] for s in range(SLOTS)], axis=1)
        total = total + lax.dot_general(
            left, right, (((1,), (1,)), ((), ())), preferred_element_type=F32
        )
    return total[:NB] + total[NB:]


def apply_kernel(fine, index, own, even, odd, values, scale, out, halo):
    fill(halo, (own, even, odd))
    field = own[0]
    product = multiply(index, halo, values, fine)
    out[...] = (scale[...] * field - SHIFT * field) + product


def last_kernel(index, own, even, odd, values, scale, u0, u1, u2, out, halo):
    fill(halo, (own, even, odd))
    field = own[0]
    product = multiply(index, halo, values, True)
    u4 = (scale[...] * field - SHIFT * field) + product
    fields = (u0[...], u1[...], u2[...], field, u4)
    lane = lax.broadcasted_iota(jnp.int32, (1, BS), 1)
    dots = jnp.zeros((1, BS), F32)
    for at, (i, j) in enumerate(PAIRS):
        dot = jnp.sum(fields[i] * fields[j], axis=(0, 1), keepdims=True)
        dots = jnp.where(lane == at, dot, dots)
    for at in range(out.shape[0]):
        out[at] = dots


def sum_kernel(parts, out):
    total = jnp.sum(parts[...], axis=0)
    for at in range(out.shape[0]):
        out[at] = total


def cholesky(gram, size):
    lower = [[None] * size for _ in range(size)]
    for j in range(size):
        pivot = gram[j][j]
        for k in range(j):
            pivot = pivot - lower[j][k] * lower[j][k]
        lower[j][j] = jnp.sqrt(pivot)
        for i in range(j + 1, size):
            entry = gram[i][j]
            for k in range(j):
                entry = entry - lower[i][k] * lower[j][k]
            lower[i][j] = entry / lower[j][j]
    return lower


def finish_kernel(parts, u0, u1, u2, u3, solution_field, hessenberg):
    total = jnp.sum(parts[...], axis=0)
    lane = lax.broadcasted_iota(jnp.int32, (NB, BS), 1)
    sublane = lax.broadcasted_iota(jnp.int32, (NB, BS), 0)
    total = jnp.broadcast_to(total, (NB, BS))
    size = ITERS + 1
    gram = [[None] * size for _ in range(size)]
    for at, (i, j) in enumerate(PAIRS):
        entry = jnp.sum(jnp.where(lane == at, total, 0.0), axis=1, keepdims=True)
        gram[i][j] = gram[j][i] = jnp.broadcast_to(entry, (NB, BS))
    lower = cholesky(gram, size)
    h = [[None] * ITERS for _ in range(size)]
    for j in range(ITERS):
        for i in range(j + 2):
            entry = lower[j + 1][i]
            if i <= j:
                entry = entry + SHIFT * lower[j][i]
            for k in range(max(i - 1, 0), j):
                entry = entry - h[i][k] * lower[j][k]
            h[i][j] = entry / lower[j][j]
    normal = [[None] * ITERS for _ in range(ITERS)]
    for i in range(ITERS):
        for j in range(i + 1):
            entry = h[0][i] * h[0][j]
            for k in range(1, j + 2):
                entry = entry + h[k][i] * h[k][j]
            normal[i][j] = entry
    factor = cholesky(normal, ITERS)
    forward = []
    for i in range(ITERS):
        entry = lower[0][0] * h[0][i]
        for k in range(i):
            entry = entry - factor[i][k] * forward[k]
        forward.append(entry / factor[i][i])
    y = [None] * ITERS
    for i in reversed(range(ITERS)):
        entry = forward[i]
        for k in range(i + 1, ITERS):
            entry = entry - factor[k][i] * y[k]
        y[i] = entry / factor[i][i]
    weights = [None] * ITERS
    for i in reversed(range(ITERS)):
        entry = y[i]
        for k in range(i + 1, ITERS):
            entry = entry - lower[k][i] * weights[k]
        weights[i] = entry / lower[i][i]
    solution_field[...] = (weights[0] * u0[...] + weights[1] * u1[...]) + (
        weights[2] * u2[...] + weights[3] * u3[...]
    )
    matrix = jnp.zeros((NB, BS), F32)
    for j in range(ITERS):
        for i in range(j + 2):
            matrix = jnp.where((sublane == i) & (lane == j), h[i][j], matrix)
    hessenberg[...] = matrix[:size, :ITERS]


SMEM = pl.BlockSpec(memory_space=pltpu.SMEM)
VMEM = pl.BlockSpec(memory_space=pltpu.VMEM)
FIELD = jax.ShapeDtypeStruct((NB, BS), F32)


def halo_index(block_columns, live_slots):
    where = block_columns.reshape(NB, SLOTS)
    live = lax.broadcasted_iota(jnp.int32, (NB, SLOTS), 1) < live_slots.reshape(NB, 1)

    def side(offset, position):
        forward = jnp.where(position % 2 == 0, 1, 2)
        return jnp.where(offset == 1, 0, jnp.where(offset == 2, forward, 3 - forward))

    row = side(where // (3 * NB), lax.axis_index(ROW))
    col = side(where // NB % 3, lax.axis_index(COL))
    return jnp.where(live, (col * 3 + row) * NB + where % NB, 9 * NB).reshape(-1)


def on_device(rows, cols, right_side, block_values, block_columns, live_slots, row_scale):
    u0 = right_side.reshape(NB, BS)
    values = block_values.reshape(NB * SLOTS, BS, BS)
    scale = row_scale.reshape(NB, BS)
    index = halo_index(block_columns, live_slots)
    halo = [pltpu.VMEM((10 * NB, BS), F32)]

    def apply(field, fine):
        return pl.pallas_call(
            lambda *refs: apply_kernel(fine, *refs),
            out_shape=FIELD,
            in_specs=[SMEM] + [VMEM] * 5,
            out_specs=VMEM,
            scratch_shapes=halo,
        )(index, *exchange(field, rows, cols), values, scale)

    u1 = apply(u0, False)
    u2 = apply(u1, True)
    u3 = apply(u2, True)
    plane = lax.axis_size(PLANE)
    depth = lax.axis_size("z")
    parts = pl.pallas_call(
        last_kernel,
        out_shape=jax.ShapeDtypeStruct((plane, 1, BS), F32),
        in_specs=[SMEM] + [VMEM] * 8,
        out_specs=VMEM,
        scratch_shapes=halo,
    )(index, *exchange(u3, rows, cols), values, scale, u0, u1, u2)
    parts = lax.all_to_all(parts, PLANE, split_axis=0, concat_axis=0, tiled=True)
    parts = pl.pallas_call(
        sum_kernel,
        out_shape=jax.ShapeDtypeStruct((depth, 1, BS), F32),
        in_specs=[VMEM],
        out_specs=VMEM,
    )(parts)
    parts = lax.all_to_all(parts, "z", split_axis=0, concat_axis=0, tiled=True)
    solution_field, hessenberg = pl.pallas_call(
        finish_kernel,
        out_shape=(FIELD, jax.ShapeDtypeStruct((ITERS + 1, ITERS), F32)),
        in_specs=[VMEM] * 5,
        out_specs=(VMEM, VMEM),
    )(parts, u0, u1, u2, u3)
    return solution_field.reshape(right_side.shape), hessenberg


def solution(mesh):
    rows, cols = mesh.shape["row"], mesh.shape["col"]
    finer = Mesh(
        mesh.devices.reshape(4, rows // 4, cols // 2, 2), ("y", "z", "x", "core")
    )
    in_specs = (
        P(ROW, COL, None, None),
        P(ROW, COL, None, None, None, None),
        P(ROW, COL, None, None),
        P(ROW, COL, None),
        P(ROW, COL, None, None),
    )
    out_specs = (P(ROW, COL, None, None), P())
    return jax.shard_map(
        lambda *arrays: on_device(rows, cols, *arrays),
        mesh=finer,
        in_specs=in_specs,
        out_specs=out_specs,
        check_vma=False,
    )
```

time: 432 us -> 143 us (0.33)
  the two profiles are of different devices: /device:TPU:32 before, /device:TPU:1 now
where the time goes in v1:
time: 143 us; the launch traced here: 142 us
  blocking collectives  59.3 us (41%)
  starting transfers between devices  55.7 us (39%)
  Pallas kernels  12 us (8%)
  waiting for transfers between devices  7.73 us (5%)
  local copies, waits for them, and re-layouts  5.53 us (4%)
    all_to_all x1, blocking collectives, on_device(): parts = lax.all_to_all(parts, 'z', split_axis=0, concat_axis=0, tiled=True)  35 us
    all_to_all x1, blocking collectives, on_device(): lax.all_to_all(parts, PLANE, split_axis=0, concat_axis=0, tiled=True)  24.3 us
    ppermute x4, starting transfers between devices, exchange(): lax.ppermute(field, ROW, even)  23.3 us
    ppermute x4, starting transfers between devices, exchange(): lax.ppermute(beside, COL, even)  15.1 us
    ppermute x4, starting transfers between devices, exchange(): lax.ppermute(beside, COL, odd)  14.3 us
    pallas_call x3, Pallas kernels, apply(): pl.pallas_call(lambda *refs: apply_kernel(fine, *refs), out_shape=FIELD,...  6.68 us
    unnamed x38, local copies, waits for them, and re-layouts  5.36 us
    ppermute x4, waiting for transfers between devices, exchange(): lax.ppermute(field, ROW, even)  4.27 us
  transfers between devices with their start and end apart: 16, of which 8 were waited for; matrix products, arithmetic and copies ran while one was open for 1% of the time, Pallas kernels for 0%

profile of v1, /device:TPU:1, one launch (start us, length us, event | category | flops | bytes accessed | tf_op | source)
XLA Modules:
  0.0 141.7 jit_solution(16156201784031855938)
XLA Ops:
  0.6 0.0 copy-start.17
  0.6 0.7 collective-permute-start.1
  1.3 7.3 %collective-permute-start = (f32[8,128]{1,0:T(8,128)}, f32[8,128]{1,0:T(8,128)S(1)}, u32[]{:S(2)}, u32[]{:S(2)}) collective-permute-start(f32[8,128]{1,0:T(8,128)} %bitcast.30), channel_id=1, source_target_pairs={{0,8},{8,0},{16,24},{24,16},{32,40},{40,32},{48,56},{56,48},{64,72... | collective-permute-start | bytes 12296 | tf_op jit(solution)/shard_map/ppermute | solution.py:33
  8.6 0.0 copy-done.17
  8.6 0.1 iota_compare_fusion
  8.7 0.1 lt.37
  8.8 0.6 copy-done.16
  9.3 0.1 copy.9
  9.4 0.1 reshape.26
  9.5 0.0 collective-permute-done.1
  9.5 0.3 collective-permute-done
  9.8 0.3 copy-done.6
  10.1 4.5 %collective-permute-start.3 = (f32[3,8,128]{2,1,0:T(8,128)S(1)}, f32[3,8,128]{2,1,0:T(8,128)S(1)}, u32[]{:S(2)}, u32[]{:S(2)}) collective-permute-start(f32[3,8,128]{2,1,0:T(8,128)S(1)} %pad_maximum_fusion.refs_1_), channel_id=1, source_target_pairs={{1,2},{2,1},{3,4},{4,3},{5,6},{6,5},{9,10},{10,9},{11,12},{12,11},... | collective-permute-start | bytes 36872 | tf_op jit(solution)/shard_map/ppermute | solution.py:39
  14.6 9.1 %collective-permute-start.2 = (f32[3,8,128]{2,1,0:T(8,128)S(1)}, f32[3,8,128]{2,1,0:T(8,128)S(1)}, u32[]{:S(2)}, u32[]{:S(2)}) collective-permute-start(f32[3,8,128]{2,1,0:T(8,128)S(1)} %pad_maximum_fusion.refs_1_), channel_id=1, source_target_pairs={{0,1},{1,0},{2,3},{3,2},{4,5},{5,4},{6,7},{7,6},{8,9},{9,8},{10,11... | collective-permute-start | bytes 36872 | tf_op jit(solution)/shard_map/ppermute | solution.py:38
  23.8 0.5 fusion.1.refs_0_.index
  24.3 0.0 collective-permute-done.3.refs_3_
  24.3 0.3 collective-permute-done.2.refs_2_
  24.6 0.0 copy-done.2
  24.6 0.3 copy-done.8
  24.9 0.3 copy-done.9
  25.2 2.2 %shard_map.68.u1 = f32[8,128]{1,0:T(8,128)} custom-call(s32[32]{0:T(128)} %fusion.1.refs_0_.index, f32[3,8,128]{2,1,0:T(8,128)} %copy-done.2, f32[3,8,128]{2,1,0:T(8,128)} %copy-done.9, f32[3,8,128]{2,1,0:T(8,128)} %copy-done.8, bf16[32,128,128]{2,1,0:T(8,128)(2,1)} %bitcast.19, f32[8,128]{1,0:T(8,128)} %bitcast.23), custom_call_target="tpu_custom_call" | custom-call | tf_op jit(solution)/shard_map/pallas_call | solution.py:194
  27.4 0.8 collective-permute-start.5
  28.2 2.9 %collective-permute-start.4 = (f32[8,128]{1,0:T(8,128)}, f32[8,128]{1,0:T(8,128)S(1)}, u32[]{:S(2)}, u32[]{:S(2)}) collective-permute-start(f32[8,128]{1,0:T(8,128)} %shard_map.68.u1), channel_id=1, source_target_pairs={{0,8},{8,0},{16,24},{24,16},{32,40},{40,32},{48,56},{56,48},{64,72... | collective-permute-start | bytes 12296 | tf_op jit(solution)/shard_map/ppermute | solution.py:33
  31.1 0.0 collective-permute-done.5
  31.1 1.6 %collective-permute-done.4 = f32[8,128]{1,0:T(8,128)S(1)} collective-permute-done((f32[8,128]{1,0:T(8,128)}, f32[8,128]{1,0:T(8,128)S(1)}, u32[]{:S(2)}, u32[]{:S(2)}) %collective-permute-start.4) | collective-permute-done | bytes 4128 | tf_op jit(solution)/shard_map/ppermute | solution.py:33
  32.8 0.0 copy-done
  32.8 1.9 %collective-permute-start.7 = (f32[3,8,128]{2,1,0:T(8,128)S(1)}, f32[3,8,128]{2,1,0:T(8,128)S(1)}, u32[]{:S(2)}, u32[]{:S(2)}) collective-permute-start(f32[3,8,128]{2,1,0:T(8,128)S(1)} %pad_maximum_fusion.1.refs_1_), channel_id=1, source_target_pairs={{1,2},{2,1},{3,4},{4,3},{5,6},{6,5},{9,10},{10,9},{11,12},{12,11},... | collective-permute-start | bytes 36872 | tf_op jit(solution)/shard_map/ppermute | solution.py:39
  34.7 2.1 %collective-permute-start.6 = (f32[3,8,128]{2,1,0:T(8,128)S(1)}, f32[3,8,128]{2,1,0:T(8,128)S(1)}, u32[]{:S(2)}, u32[]{:S(2)}) collective-permute-start(f32[3,8,128]{2,1,0:T(8,128)S(1)} %pad_maximum_fusion.1.refs_1_), channel_id=1, source_target_pairs={{0,1},{1,0},{2,3},{3,2},{4,5},{5,4},{6,7},{7,6},{8,9},{9,8},{10,11... | collective-permute-start | bytes 36872 | tf_op jit(solution)/shard_map/ppermute | solution.py:38
  36.9 0.9 collective-permute-done.7.refs_3_
  37.8 0.0 collective-permute-done.6.refs_2_
  37.8 0.0 copy-done.4
  37.8 0.6 copy-done.11
  38.4 0.6 copy-done.14
  39.0 2.2 %shard_map.69.u2 = f32[8,128]{1,0:T(8,128)} custom-call(s32[32]{0:T(128)} %fusion.1.refs_0_.index, f32[3,8,128]{2,1,0:T(8,128)} %copy-done.4, f32[3,8,128]{2,1,0:T(8,128)} %copy-done.14, f32[3,8,128]{2,1,0:T(8,128)} %copy-done.11, bf16[32,128,128]{2,1,0:T(8,128)(2,1)} %bitcast.20, f32[8,128]{1,0:T(8,128)} %bitcast.24), custom_call_target="tpu_custom_call" | custom-call | tf_op jit(solution)/shard_map/pallas_call | solution.py:194
  41.2 0.8 collective-permute-start.9
  42.0 5.6 %collective-permute-start.8 = (f32[8,128]{1,0:T(8,128)}, f32[8,128]{1,0:T(8,128)S(1)}, u32[]{:S(2)}, u32[]{:S(2)}) collective-permute-start(f32[8,128]{1,0:T(8,128)} %shard_map.69.u2), channel_id=1, source_target_pairs={{0,8},{8,0},{16,24},{24,16},{32,40},{40,32},{48,56},{56,48},{64,72... | collective-permute-start | bytes 12296 | tf_op jit(solution)/shard_map/ppermute | solution.py:33
  47.6 0.0 collective-permute-done.9
  47.6 1.2 collective-permute-done.8
  48.8 0.0 copy-done.1
  48.8 4.2 %collective-permute-start.11 = (f32[3,8,128]{2,1,0:T(8,128)S(1)}, f32[3,8,128]{2,1,0:T(8,128)S(1)}, u32[]{:S(2)}, u32[]{:S(2)}) collective-permute-start(f32[3,8,128]{2,1,0:T(8,128)S(1)} %pad_maximum_fusion.2.refs_1_), channel_id=1, source_target_pairs={{1,2},{2,1},{3,4},{4,3},{5,6},{6,5},{9,10},{10,9},{11,12},{12,11},... | collective-permute-start | bytes 36872 | tf_op jit(solution)/shard_map/ppermute | solution.py:39
  53.0 1.9 %collective-permute-start.10 = (f32[3,8,128]{2,1,0:T(8,128)S(1)}, f32[3,8,128]{2,1,0:T(8,128)S(1)}, u32[]{:S(2)}, u32[]{:S(2)}) collective-permute-start(f32[3,8,128]{2,1,0:T(8,128)S(1)} %pad_maximum_fusion.2.refs_1_), channel_id=1, source_target_pairs={{0,1},{1,0},{2,3},{3,2},{4,5},{5,4},{6,7},{7,6},{8,9},{9,8},{10,11... | collective-permute-start | bytes 36872 | tf_op jit(solution)/shard_map/ppermute | solution.py:38
  54.9 0.0 collective-permute-done.11.refs_3_
  54.9 0.0 copy-start.12
  54.9 1.1 collective-permute-done.10.refs_2_
  56.1 0.0 copy-done.5
  56.1 0.0 copy-done.12
  56.1 0.6 copy-done.15
  56.7 2.2 %shard_map.70.u3 = f32[8,128]{1,0:T(8,128)} custom-call(s32[32]{0:T(128)} %fusion.1.refs_0_.index, f32[3,8,128]{2,1,0:T(8,128)} %copy-done.5, f32[3,8,128]{2,1,0:T(8,128)} %copy-done.15, f32[3,8,128]{2,1,0:T(8,128)} %copy-done.12, bf16[32,128,128]{2,1,0:T(8,128)(2,1)} %bitcast.21, f32[8,128]{1,0:T(8,128)} %bitcast.25), custom_call_target="tpu_custom_call" | custom-call | tf_op jit(solution)/shard_map/pallas_call | solution.py:194
  58.9 0.8 collective-permute-start.13
  59.7 7.5 %collective-permute-start.12 = (f32[8,128]{1,0:T(8,128)}, f32[8,128]{1,0:T(8,128)S(1)}, u32[]{:S(2)}, u32[]{:S(2)}) collective-permute-start(f32[8,128]{1,0:T(8,128)} %shard_map.70.u3), channel_id=1, source_target_pairs={{0,8},{8,0},{16,24},{24,16},{32,40},{40,32},{48,56},{56,48},{64,72... | collective-permute-start | bytes 12296 | tf_op jit(solution)/shard_map/ppermute | solution.py:33
  67.2 0.0 collective-permute-done.13
  67.2 1.2 collective-permute-done.12
  68.4 3.7 %collective-permute-start.15 = (f32[3,8,128]{2,1,0:T(8,128)S(1)}, f32[3,8,128]{2,1,0:T(8,128)S(1)}, u32[]{:S(2)}, u32[]{:S(2)}) collective-permute-start(f32[3,8,128]{2,1,0:T(8,128)S(1)} %pad_maximum_fusion.3.own), channel_id=1, source_target_pairs={{1,2},{2,1},{3,4},{4,3},{5,6},{6,5},{9,10},{10,9},{11,12},{12,11},... | collective-permute-start | bytes 36872 | tf_op jit(solution)/shard_map/ppermute | solution.py:39
  72.1 1.9 %collective-permute-start.14 = (f32[3,8,128]{2,1,0:T(8,128)S(1)}, f32[3,8,128]{2,1,0:T(8,128)S(1)}, u32[]{:S(2)}, u32[]{:S(2)}) collective-permute-start(f32[3,8,128]{2,1,0:T(8,128)S(1)} %pad_maximum_fusion.3.own), channel_id=1, source_target_pairs={{0,1},{1,0},{2,3},{3,2},{4,5},{5,4},{6,7},{7,6},{8,9},{9,8},{10,11... | collective-permute-start | bytes 36872 | tf_op jit(solution)/shard_map/ppermute | solution.py:38
  74.0 0.0 collective-permute-done.15.odd
  74.0 1.1 collective-permute-done.14.even
  75.2 0.0 copy-done.3
  75.2 0.6 copy-done.13
  75.8 2.4 %shard_map.71 = f32[32,1,128]{2,1,0:T(1,128)} custom-call(s32[32]{0:T(128)} %fusion.1.refs_0_.index, f32[3,8,128]{2,1,0:T(8,128)} %copy-done.3, f32[3,8,128]{2,1,0:T(8,128)} %copy-done.13, f32[3,8,128]{2,1,0:T(8,128)} %copy-done.10, bf16[32,128,128]{2,1,0:T(8,128)(2,1)} %bitcast.22, f32[8,128]{1,0:T(8,128)} %bitcast.26, f32[8,128]{1,0:T(8,128)} %bitcast.31, ...), custom_call_target="tpu_custom_call" | custom-call | tf_op jit(solution)/shard_map/pallas_call | solution.py:207
  78.1 24.3 %all_to_all.10.parts = f32[32,1,128]{2,1,0:T(1,128)} all-to-all(f32[32,1,128]{2,1,0:T(1,128)} %shard_map.71), channel_id=1, replica_groups=mesh['y'=4,'z'=32,'x'=4,'core'=2] {'y','x','core'}, dimensions={0} | all-to-all | bytes 32768 | tf_op jit(solution)/shard_map/all_to_all | solution.py:214
  102.4 1.4 shard_map.72
  103.8 35.0 %all_to_all.11.parts = f32[32,1,128]{2,1,0:T(1,128)} all-to-all(f32[32,1,128]{2,1,0:T(1,128)} %shard_map.72), channel_id=1, replica_groups=mesh['y'=4,'z'=32,'x'=4,'core'=2] {'z'}, dimensions={0} | all-to-all | bytes 32768 | tf_op jit(solution)/shard_map/all_to_all | solution.py:221
  138.8 1.6 %shard_map.73 = (f32[8,128]{1,0:T(8,128)}, f32[5,4]{1,0:T(8,128)}) custom-call(f32[32,1,128]{2,1,0:T(1,128)} %all_to_all.11.parts, f32[8,128]{1,0:T(8,128)} %bitcast.32, f32[8,128]{1,0:T(8,128)} %shard_map.68.u1, f32[8,128]{1,0:T(8,128)} %shard_map.69.u2, f32[8,128]{1,0:T(8,128)} %shard_map.70.u3), custom_call_target="tpu_custom_call" | custom-call | tf_op jit(solution)/shard_map/pallas_call | solution.py:222
  140.3 1.3 copy.10
  (22 shorter events, 0.0 us)
Async XLA Ops:
  0.6 8.0 %copy-start.17 = (s32[1,1,8]{2,1,0:T(1,128)S(1)}, s32[1,1,8]{2,1,0:T(1,128)}, u32[]{:S(2)}) copy-start(s32[1,1,8]{2,1,0:T(1,128)} %param.8) | copy-start | bytes 100
  0.6 8.9 %collective-permute-start.1 = (f32[8,128]{1,0:T(8,128)}, f32[8,128]{1,0:T(8,128)S(1)}, u32[]{:S(2)}, u32[]{:S(2)}) collective-permute-start(f32[8,128]{1,0:T(8,128)} %bitcast.29), channel_id=1, source_target_pairs={{8,16},{16,8},{24,32},{32,24},{40,48},{48,40},{56,64},{64,56},{72,... | collective-permute-start | bytes 12296 | tf_op jit(solution)/shard_map/ppermute | solution.py:33
  1.3 8.5 %collective-permute-start = (f32[8,128]{1,0:T(8,128)}, f32[8,128]{1,0:T(8,128)S(1)}, u32[]{:S(2)}, u32[]{:S(2)}) collective-permute-start(f32[8,128]{1,0:T(8,128)} %bitcast.30), channel_id=1, source_target_pairs={{0,8},{8,0},{16,24},{24,16},{32,40},{40,32},{48,56},{56,48},{64,72... | collective-permute-start | bytes 12296 | tf_op jit(solution)/shard_map/ppermute | solution.py:33
  8.7 0.7 copy-start.16
  9.4 0.7 copy-start.6
  10.1 14.5 %copy-start.2 = (f32[3,8,128]{2,1,0:T(8,128)}, f32[3,8,128]{2,1,0:T(8,128)S(1)}, u32[]{:S(2)}) copy-start(f32[3,8,128]{2,1,0:T(8,128)S(1)} %pad_maximum_fusion.refs_1_) | copy-start | bytes 36868
  10.1 14.2 %collective-permute-start.3 = (f32[3,8,128]{2,1,0:T(8,128)S(1)}, f32[3,8,128]{2,1,0:T(8,128)S(1)}, u32[]{:S(2)}, u32[]{:S(2)}) collective-permute-start(f32[3,8,128]{2,1,0:T(8,128)S(1)} %pad_maximum_fusion.refs_1_), channel_id=1, source_target_pairs={{1,2},{2,1},{3,4},{4,3},{5,6},{6,5},{9,10},{10,9},{11,12},{12,11},... | collective-permute-start | bytes 36872 | tf_op jit(solution)/shard_map/ppermute | solution.py:39
  14.6 10.0 %collective-permute-start.2 = (f32[3,8,128]{2,1,0:T(8,128)S(1)}, f32[3,8,128]{2,1,0:T(8,128)S(1)}, u32[]{:S(2)}, u32[]{:S(2)}) collective-permute-start(f32[3,8,128]{2,1,0:T(8,128)S(1)} %pad_maximum_fusion.refs_1_), channel_id=1, source_target_pairs={{0,1},{1,0},{2,3},{3,2},{4,5},{5,4},{6,7},{7,6},{8,9},{9,8},{10,11... | collective-permute-start | bytes 36872 | tf_op jit(solution)/shard_map/ppermute | solution.py:38
  24.3 0.6 copy-start.8
  24.6 0.6 copy-start.9
  27.4 5.4 %copy-start = (f32[8,128]{1,0:T(8,128)S(1)}, f32[8,128]{1,0:T(8,128)}, u32[]{:S(2)}) copy-start(f32[8,128]{1,0:T(8,128)} %shard_map.68.u1) | copy-start | bytes 12292
  27.4 3.7 %collective-permute-start.5 = (f32[8,128]{1,0:T(8,128)}, f32[8,128]{1,0:T(8,128)S(1)}, u32[]{:S(2)}, u32[]{:S(2)}) collective-permute-start(f32[8,128]{1,0:T(8,128)} %shard_map.68.u1), channel_id=1, source_target_pairs={{8,16},{16,8},{24,32},{32,24},{40,48},{48,40},{56,64},{64,56},{72,... | collective-permute-start | bytes 12296 | tf_op jit(solution)/shard_map/ppermute | solution.py:33
  28.2 4.6 %collective-permute-start.4 = (f32[8,128]{1,0:T(8,128)}, f32[8,128]{1,0:T(8,128)S(1)}, u32[]{:S(2)}, u32[]{:S(2)}) collective-permute-start(f32[8,128]{1,0:T(8,128)} %shard_map.68.u1), channel_id=1, source_target_pairs={{0,8},{8,0},{16,24},{24,16},{32,40},{40,32},{48,56},{56,48},{64,72... | collective-permute-start | bytes 12296 | tf_op jit(solution)/shard_map/ppermute | solution.py:33
  32.8 5.0 %copy-start.4 = (f32[3,8,128]{2,1,0:T(8,128)}, f32[3,8,128]{2,1,0:T(8,128)S(1)}, u32[]{:S(2)}) copy-start(f32[3,8,128]{2,1,0:T(8,128)S(1)} %pad_maximum_fusion.1.refs_1_) | copy-start | bytes 36868
  32.8 5.0 %collective-permute-start.7 = (f32[3,8,128]{2,1,0:T(8,128)S(1)}, f32[3,8,128]{2,1,0:T(8,128)S(1)}, u32[]{:S(2)}, u32[]{:S(2)}) collective-permute-start(f32[3,8,128]{2,1,0:T(8,128)S(1)} %pad_maximum_fusion.1.refs_1_), channel_id=1, source_target_pairs={{1,2},{2,1},{3,4},{4,3},{5,6},{6,5},{9,10},{10,9},{11,12},{12,11},... | collective-permute-start | bytes 36872 | tf_op jit(solution)/shard_map/ppermute | solution.py:39
  34.7 3.1 %collective-permute-start.6 = (f32[3,8,128]{2,1,0:T(8,128)S(1)}, f32[3,8,128]{2,1,0:T(8,128)S(1)}, u32[]{:S(2)}, u32[]{:S(2)}) collective-permute-start(f32[3,8,128]{2,1,0:T(8,128)S(1)} %pad_maximum_fusion.1.refs_1_), channel_id=1, source_target_pairs={{0,1},{1,0},{2,3},{3,2},{4,5},{5,4},{6,7},{7,6},{8,9},{9,8},{10,11... | collective-permute-start | bytes 36872 | tf_op jit(solution)/shard_map/ppermute | solution.py:38
  37.8 0.6 copy-start.11
  38.4 0.6 copy-start.14
  41.2 7.6 %copy-start.1 = (f32[8,128]{1,0:T(8,128)S(1)}, f32[8,128]{1,0:T(8,128)}, u32[]{:S(2)}) copy-start(f32[8,128]{1,0:T(8,128)} %shard_map.69.u2) | copy-start | bytes 12292
  41.2 6.4 %collective-permute-start.9 = (f32[8,128]{1,0:T(8,128)}, f32[8,128]{1,0:T(8,128)S(1)}, u32[]{:S(2)}, u32[]{:S(2)}) collective-permute-start(f32[8,128]{1,0:T(8,128)} %shard_map.69.u2), channel_id=1, source_target_pairs={{8,16},{16,8},{24,32},{32,24},{40,48},{48,40},{56,64},{64,56},{72,... | collective-permute-start | bytes 12296 | tf_op jit(solution)/shard_map/ppermute | solution.py:33
  42.0 6.8 %collective-permute-start.8 = (f32[8,128]{1,0:T(8,128)}, f32[8,128]{1,0:T(8,128)S(1)}, u32[]{:S(2)}, u32[]{:S(2)}) collective-permute-start(f32[8,128]{1,0:T(8,128)} %shard_map.69.u2), channel_id=1, source_target_pairs={{0,8},{8,0},{16,24},{24,16},{32,40},{40,32},{48,56},{56,48},{64,72... | collective-permute-start | bytes 12296 | tf_op jit(solution)/shard_map/ppermute | solution.py:33
  48.8 7.3 %copy-start.5 = (f32[3,8,128]{2,1,0:T(8,128)}, f32[3,8,128]{2,1,0:T(8,128)S(1)}, u32[]{:S(2)}) copy-start(f32[3,8,128]{2,1,0:T(8,128)S(1)} %pad_maximum_fusion.2.refs_1_) | copy-start | bytes 36868
  48.8 6.1 %collective-permute-start.11 = (f32[3,8,128]{2,1,0:T(8,128)S(1)}, f32[3,8,128]{2,1,0:T(8,128)S(1)}, u32[]{:S(2)}, u32[]{:S(2)}) collective-permute-start(f32[3,8,128]{2,1,0:T(8,128)S(1)} %pad_maximum_fusion.2.refs_1_), channel_id=1, source_target_pairs={{1,2},{2,1},{3,4},{4,3},{5,6},{6,5},{9,10},{10,9},{11,12},{12,11},... | collective-permute-start | bytes 36872 | tf_op jit(solution)/shard_map/ppermute | solution.py:39
  53.0 3.1 %collective-permute-start.10 = (f32[3,8,128]{2,1,0:T(8,128)S(1)}, f32[3,8,128]{2,1,0:T(8,128)S(1)}, u32[]{:S(2)}, u32[]{:S(2)}) collective-permute-start(f32[3,8,128]{2,1,0:T(8,128)S(1)} %pad_maximum_fusion.2.refs_1_), channel_id=1, source_target_pairs={{0,1},{1,0},{2,3},{3,2},{4,5},{5,4},{6,7},{7,6},{8,9},{9,8},{10,11... | collective-permute-start | bytes 36872 | tf_op jit(solution)/shard_map/ppermute | solution.py:38
  54.9 1.1 copy-start.12
  56.1 0.6 copy-start.15
  58.9 9.5 %copy-start.7 = (f32[8,128]{1,0:T(8,128)S(1)}, f32[8,128]{1,0:T(8,128)}, u32[]{:S(2)}) copy-start(f32[8,128]{1,0:T(8,128)} %shard_map.70.u3) | copy-start | bytes 12292
  58.9 8.3 %collective-permute-start.13 = (f32[8,128]{1,0:T(8,128)}, f32[8,128]{1,0:T(8,128)S(1)}, u32[]{:S(2)}, u32[]{:S(2)}) collective-permute-start(f32[8,128]{1,0:T(8,128)} %shard_map.70.u3), channel_id=1, source_target_pairs={{8,16},{16,8},{24,32},{32,24},{40,48},{48,40},{56,64},{64,56},{72,... | collective-permute-start | bytes 12296 | tf_op jit(solution)/shard_map/ppermute | solution.py:33
  59.7 8.7 %collective-permute-start.12 = (f32[8,128]{1,0:T(8,128)}, f32[8,128]{1,0:T(8,128)S(1)}, u32[]{:S(2)}, u32[]{:S(2)}) collective-permute-start(f32[8,128]{1,0:T(8,128)} %shard_map.70.u3), channel_id=1, source_target_pairs={{0,8},{8,0},{16,24},{24,16},{32,40},{40,32},{48,56},{56,48},{64,72... | collective-permute-start | bytes 12296 | tf_op jit(solution)/shard_map/ppermute | solution.py:33
  68.4 6.8 %copy-start.3 = (f32[3,8,128]{2,1,0:T(8,128)}, f32[3,8,128]{2,1,0:T(8,128)S(1)}, u32[]{:S(2)}) copy-start(f32[3,8,128]{2,1,0:T(8,128)S(1)} %pad_maximum_fusion.3.own) | copy-start | bytes 36868
  68.4 5.6 %collective-permute-start.15 = (f32[3,8,128]{2,1,0:T(8,128)S(1)}, f32[3,8,128]{2,1,0:T(8,128)S(1)}, u32[]{:S(2)}, u32[]{:S(2)}) collective-permute-start(f32[3,8,128]{2,1,0:T(8,128)S(1)} %pad_maximum_fusion.3.own), channel_id=1, source_target_pairs={{1,2},{2,1},{3,4},{4,3},{5,6},{6,5},{9,10},{10,9},{11,12},{12,11},... | collective-permute-start | bytes 36872 | tf_op jit(solution)/shard_map/ppermute | solution.py:39
  72.1 3.1 %collective-permute-start.14 = (f32[3,8,128]{2,1,0:T(8,128)S(1)}, f32[3,8,128]{2,1,0:T(8,128)S(1)}, u32[]{:S(2)}, u32[]{:S(2)}) collective-permute-start(f32[3,8,128]{2,1,0:T(8,128)S(1)} %pad_maximum_fusion.3.own), channel_id=1, source_target_pairs={{0,1},{1,0},{2,3},{3,2},{4,5},{5,4},{6,7},{7,6},{8,9},{9,8},{10,11... | collective-permute-start | bytes 36872 | tf_op jit(solution)/shard_map/ppermute | solution.py:38
  74.0 1.1 copy-start.10
  75.2 0.6 copy-start.13

commit v2 on v1

--- a/solution.py
+++ b/solution.py
@@ -161,12 +161,13 @@
     matrix = jnp.zeros((NB, BS), F32)
     for j in range(ITERS):
         for i in range(j + 2):
-            matrix = jnp.where((sublane == i) & (lane == j), h[i][j], matrix)
-    hessenberg[...] = matrix[:size, :ITERS]
+            matrix = jnp.where((sublane == j) & (lane == i), h[i][j], matrix)
+    hessenberg[...] = matrix[:ITERS, :size]
 
 
 SMEM = pl.BlockSpec(memory_space=pltpu.SMEM)
 VMEM = pl.BlockSpec(memory_space=pltpu.VMEM)
+PARAMS = pltpu.CompilerParams(vmem_limit_bytes=4 << 20)
 FIELD = jax.ShapeDtypeStruct((NB, BS), F32)
 
 
@@ -197,6 +198,7 @@
             in_specs=[SMEM] + [VMEM] * 5,
             out_specs=VMEM,
             scratch_shapes=halo,
+            compiler_params=PARAMS,
         )(index, *exchange(field, rows, cols), values, scale)
 
     u1 = apply(u0, False)
@@ -210,6 +212,7 @@
         in_specs=[SMEM] + [VMEM] * 8,
         out_specs=VMEM,
         scratch_shapes=halo,
+        compiler_params=PARAMS,
     )(index, *exchange(u3, rows, cols), values, scale, u0, u1, u2)
     parts = lax.all_to_all(parts, PLANE, split_axis=0, concat_axis=0, tiled=True)
     parts = pl.pallas_call(
@@ -217,15 +220,17 @@
         out_shape=jax.ShapeDtypeStruct((depth, 1, BS), F32),
         in_specs=[VMEM],
         out_specs=VMEM,
+        compiler_params=PARAMS,
     )(parts)
     parts = lax.all_to_all(parts, "z", split_axis=0, concat_axis=0, tiled=True)
     solution_field, hessenberg = pl.pallas_call(
         finish_kernel,
-        out_shape=(FIELD, jax.ShapeDtypeStruct((ITERS + 1, ITERS), F32)),
+        out_shape=(FIELD, jax.ShapeDtypeStruct((ITERS, ITERS + 1), F32)),
         in_specs=[VMEM] * 5,
         out_specs=(VMEM, VMEM),
+        compiler_params=PARAMS,
     )(parts, u0, u1, u2, u3)
-    return solution_field.reshape(right_side.shape), hessenberg
+    return solution_field.reshape(right_side.shape), hessenberg.T
 
 
 def solution(mesh):

time: 143 us -> 130 us (0.909)
  Pallas kernels: 12 us -> 4.66 us
  local copies, waits for them, and re-layouts: 5.53 us -> 2.42 us
    pallas_call x3, Pallas kernels: 6.68 us -> 2.73 us  [apply(): pl.pallas_call(lambda *refs: apply_kernel(fine, *refs), out_shape=FIELD,...]
    unnamed x38 -> x13, local copies, waits for them, and re-layouts: 5.36 us -> 2.25 us
  transfers between devices with their start and end apart: 16 -> 16, of which waited for: 8 -> 8; matrix products, arithmetic and copies ran while one was open for 1% -> 0% of each run, Pallas kernels for 0% -> 0%
where the time goes in v2:
time: 130 us; the launch traced here: 129 us
  blocking collectives  58.1 us (45%)
  starting transfers between devices  55.3 us (43%)
  waiting for transfers between devices  7.62 us (6%)
  Pallas kernels  4.66 us (4%)
  local copies, waits for them, and re-layouts  2.42 us (2%)
    all_to_all x1, blocking collectives, on_device(): parts = lax.all_to_all(parts, 'z', split_axis=0, concat_axis=0, tiled=True)  34.5 us
    ppermute x4, starting transfers between devices, exchange(): lax.ppermute(field, ROW, even)  23.8 us
    all_to_all x1, blocking collectives, on_device(): lax.all_to_all(parts, PLANE, split_axis=0, concat_axis=0, tiled=True)  23.6 us
    ppermute x4, starting transfers between devices, exchange(): lax.ppermute(beside, COL, even)  15.1 us
    ppermute x4, starting transfers between devices, exchange(): lax.ppermute(beside, COL, odd)  13.6 us
    ppermute x4, waiting for transfers between devices, exchange(): lax.ppermute(field, ROW, even)  3.64 us
    ppermute x4, waiting for transfers between devices, exchange(): lax.ppermute(beside, COL, even)  3.04 us
    pallas_call x3, Pallas kernels, apply(): pl.pallas_call(lambda *refs: apply_kernel(fine, *refs), out_shape=FIELD,...  2.73 us
  transfers between devices with their start and end apart: 16, of which 8 were waited for; matrix products, arithmetic and copies ran while one was open for 0% of the time, Pallas kernels for 0%

profile of v2, /device:TPU:1, one launch (start us, length us, event | category | flops | bytes accessed | tf_op | source)
XLA Modules:
  0.0 129.1 jit_solution(3490397792760168719)
XLA Ops:
  0.6 0.0 copy-start.5
  0.6 0.7 collective-permute-start.1
  1.3 7.3 %collective-permute-start = (f32[8,128]{1,0:T(8,128)}, f32[8,128]{1,0:T(8,128)S(1)}, u32[]{:S(2)}, u32[]{:S(2)}) collective-permute-start(f32[8,128]{1,0:T(8,128)} %bitcast.31), channel_id=1, source_target_pairs={{0,8},{8,0},{16,24},{24,16},{32,40},{40,32},{48,56},{56,48},{64,72... | collective-permute-start | bytes 12296 | tf_op jit(solution)/shard_map/ppermute | solution.py:33
  8.6 0.0 copy-done.5
  8.6 0.1 iota_compare_fusion
  8.7 0.0 copy-start.4
  8.7 0.1 lt.37
  8.8 0.6 copy-done.4
  9.3 0.1 copy.8
  9.4 0.0 copy-start.3
  9.4 0.1 reshape.26
  9.5 0.0 collective-permute-done.1
  9.5 0.3 collective-permute-done
  9.8 0.3 copy-done.3
  10.1 0.0 copy-start.2
  10.1 4.5 %collective-permute-start.3 = (f32[3,8,128]{2,1,0:T(8,128)S(1)}, f32[3,8,128]{2,1,0:T(8,128)S(1)}, u32[]{:S(2)}, u32[]{:S(2)}) collective-permute-start(f32[3,8,128]{2,1,0:T(8,128)S(1)} %pad_maximum_fusion.refs_1_), channel_id=1, source_target_pairs={{1,2},{2,1},{3,4},{4,3},{5,6},{6,5},{9,10},{10,9},{11,12},{12,11},... | collective-permute-start | bytes 36872 | tf_op jit(solution)/shard_map/ppermute | solution.py:39
  14.6 9.1 %collective-permute-start.2 = (f32[3,8,128]{2,1,0:T(8,128)S(1)}, f32[3,8,128]{2,1,0:T(8,128)S(1)}, u32[]{:S(2)}, u32[]{:S(2)}) collective-permute-start(f32[3,8,128]{2,1,0:T(8,128)S(1)} %pad_maximum_fusion.refs_1_), channel_id=1, source_target_pairs={{0,1},{1,0},{2,3},{3,2},{4,5},{5,4},{6,7},{7,6},{8,9},{9,8},{10,11... | collective-permute-start | bytes 36872 | tf_op jit(solution)/shard_map/ppermute | solution.py:38
  23.8 0.0 collective-permute-done.3.refs_3_
  23.8 0.8 collective-permute-done.2.refs_2_
  24.6 0.0 copy-done.2
  24.6 0.0 copy-start
  24.6 1.2 copy-done
  25.8 0.0 copy-start.1
  25.8 0.9 shard_map.68.u1
  26.7 0.7 collective-permute-start.5
  27.4 2.9 %collective-permute-start.4 = (f32[8,128]{1,0:T(8,128)S(1)}, f32[8,128]{1,0:T(8,128)S(1)}, u32[]{:S(2)}, u32[]{:S(2)}) collective-permute-start(f32[8,128]{1,0:T(8,128)S(1)} %shard_map.68.u1), channel_id=1, source_target_pairs={{0,8},{8,0},{16,24},{24,16},{32,40},{40,32},{48,56},{56,48},{64,72... | collective-permute-start | bytes 12296 | tf_op jit(solution)/shard_map/ppermute | solution.py:33
  30.3 0.0 collective-permute-done.5
  30.3 1.4 %collective-permute-done.4 = f32[8,128]{1,0:T(8,128)S(1)} collective-permute-done((f32[8,128]{1,0:T(8,128)S(1)}, f32[8,128]{1,0:T(8,128)S(1)}, u32[]{:S(2)}, u32[]{:S(2)}) %collective-permute-start.4) | collective-permute-done | bytes 4128 | tf_op jit(solution)/shard_map/ppermute | solution.py:33
  31.8 1.9 %collective-permute-start.7 = (f32[3,8,128]{2,1,0:T(8,128)S(1)}, f32[3,8,128]{2,1,0:T(8,128)S(1)}, u32[]{:S(2)}, u32[]{:S(2)}) collective-permute-start(f32[3,8,128]{2,1,0:T(8,128)S(1)} %pad_maximum_fusion.1.refs_1_), channel_id=1, source_target_pairs={{1,2},{2,1},{3,4},{4,3},{5,6},{6,5},{9,10},{10,9},{11,12},{12,11},... | collective-permute-start | bytes 36872 | tf_op jit(solution)/shard_map/ppermute | solution.py:39
  33.7 2.1 %collective-permute-start.6 = (f32[3,8,128]{2,1,0:T(8,128)S(1)}, f32[3,8,128]{2,1,0:T(8,128)S(1)}, u32[]{:S(2)}, u32[]{:S(2)}) collective-permute-start(f32[3,8,128]{2,1,0:T(8,128)S(1)} %pad_maximum_fusion.1.refs_1_), channel_id=1, source_target_pairs={{0,1},{1,0},{2,3},{3,2},{4,5},{5,4},{6,7},{7,6},{8,9},{9,8},{10,11... | collective-permute-start | bytes 36872 | tf_op jit(solution)/shard_map/ppermute | solution.py:38
  35.8 0.9 collective-permute-done.7.refs_3_
  36.8 0.0 collective-permute-done.6.refs_2_
  36.8 0.0 copy-done.1
  36.8 0.9 shard_map.69.u2
  37.7 0.7 collective-permute-start.9
  38.4 6.2 %collective-permute-start.8 = (f32[8,128]{1,0:T(8,128)S(1)}, f32[8,128]{1,0:T(8,128)S(1)}, u32[]{:S(2)}, u32[]{:S(2)}) collective-permute-start(f32[8,128]{1,0:T(8,128)S(1)} %shard_map.69.u2), channel_id=1, source_target_pairs={{0,8},{8,0},{16,24},{24,16},{32,40},{40,32},{48,56},{56,48},{64,72... | collective-permute-start | bytes 12296 | tf_op jit(solution)/shard_map/ppermute | solution.py:33
  44.6 0.0 collective-permute-done.9
  44.6 1.0 collective-permute-done.8
  45.6 4.2 %collective-permute-start.11 = (f32[3,8,128]{2,1,0:T(8,128)S(1)}, f32[3,8,128]{2,1,0:T(8,128)S(1)}, u32[]{:S(2)}, u32[]{:S(2)}) collective-permute-start(f32[3,8,128]{2,1,0:T(8,128)S(1)} %pad_maximum_fusion.2.refs_1_), channel_id=1, source_target_pairs={{1,2},{2,1},{3,4},{4,3},{5,6},{6,5},{9,10},{10,9},{11,12},{12,11},... | collective-permute-start | bytes 36872 | tf_op jit(solution)/shard_map/ppermute | solution.py:39
  49.7 1.9 %collective-permute-start.10 = (f32[3,8,128]{2,1,0:T(8,128)S(1)}, f32[3,8,128]{2,1,0:T(8,128)S(1)}, u32[]{:S(2)}, u32[]{:S(2)}) collective-permute-start(f32[3,8,128]{2,1,0:T(8,128)S(1)} %pad_maximum_fusion.2.refs_1_), channel_id=1, source_target_pairs={{0,1},{1,0},{2,3},{3,2},{4,5},{5,4},{6,7},{7,6},{8,9},{9,8},{10,11... | collective-permute-start | bytes 36872 | tf_op jit(solution)/shard_map/ppermute | solution.py:38
  51.7 0.0 collective-permute-done.11.refs_3_
  51.7 1.1 collective-permute-done.10.refs_2_
  52.8 0.9 shard_map.70.u3
  53.7 0.7 collective-permute-start.13
  54.4 7.5 %collective-permute-start.12 = (f32[8,128]{1,0:T(8,128)S(1)}, f32[8,128]{1,0:T(8,128)S(1)}, u32[]{:S(2)}, u32[]{:S(2)}) collective-permute-start(f32[8,128]{1,0:T(8,128)S(1)} %shard_map.70.u3), channel_id=1, source_target_pairs={{0,8},{8,0},{16,24},{24,16},{32,40},{40,32},{48,56},{56,48},{64,72... | collective-permute-start | bytes 12296 | tf_op jit(solution)/shard_map/ppermute | solution.py:33
  61.9 0.0 collective-permute-done.13
  61.9 1.0 collective-permute-done.12
  62.9 3.1 %collective-permute-start.15 = (f32[3,8,128]{2,1,0:T(8,128)S(1)}, f32[3,8,128]{2,1,0:T(8,128)S(1)}, u32[]{:S(2)}, u32[]{:S(2)}) collective-permute-start(f32[3,8,128]{2,1,0:T(8,128)S(1)} %pad_maximum_fusion.3.own), channel_id=1, source_target_pairs={{1,2},{2,1},{3,4},{4,3},{5,6},{6,5},{9,10},{10,9},{11,12},{12,11},... | collective-permute-start | bytes 36872 | tf_op jit(solution)/shard_map/ppermute | solution.py:39
  66.0 1.9 %collective-permute-start.14 = (f32[3,8,128]{2,1,0:T(8,128)S(1)}, f32[3,8,128]{2,1,0:T(8,128)S(1)}, u32[]{:S(2)}, u32[]{:S(2)}) collective-permute-start(f32[3,8,128]{2,1,0:T(8,128)S(1)} %pad_maximum_fusion.3.own), channel_id=1, source_target_pairs={{0,1},{1,0},{2,3},{3,2},{4,5},{5,4},{6,7},{7,6},{8,9},{9,8},{10,11... | collective-permute-start | bytes 36872 | tf_op jit(solution)/shard_map/ppermute | solution.py:38
  67.9 0.0 collective-permute-done.15.odd
  67.9 1.1 collective-permute-done.14.even
  69.0 1.1 shard_map.71
  70.1 23.6 %all_to_all.10.parts = f32[32,1,128]{2,1,0:T(1,128)S(1)} all-to-all(f32[32,1,128]{2,1,0:T(1,128)S(1)} %shard_map.71), channel_id=1, replica_groups=mesh['y'=4,'z'=32,'x'=4,'core'=2] {'y','x','core'}, dimensions={0} | all-to-all | bytes 32768 | tf_op jit(solution)/shard_map/all_to_all | solution.py:217
  93.7 34.5 %all_to_all.11.parts = f32[32,1,128]{2,1,0:T(1,128)S(1)} all-to-all(f32[32,1,128]{2,1,0:T(1,128)S(1)} %shard_map.72), channel_id=1, replica_groups=mesh['y'=4,'z'=32,'x'=4,'core'=2] {'z'}, dimensions={0} | all-to-all | bytes 32768 | tf_op jit(solution)/shard_map/all_to_all | solution.py:225
  128.3 0.8 shard_map.73
  (6 shorter events, 0.1 us)
Async XLA Ops:
  0.6 8.0 %copy-start.5 = (s32[1,1,8]{2,1,0:T(1,128)S(1)}, s32[1,1,8]{2,1,0:T(1,128)}, u32[]{:S(2)}) copy-start(s32[1,1,8]{2,1,0:T(1,128)} %param.8) | copy-start | bytes 100
  0.6 8.9 %collective-permute-start.1 = (f32[8,128]{1,0:T(8,128)}, f32[8,128]{1,0:T(8,128)S(1)}, u32[]{:S(2)}, u32[]{:S(2)}) collective-permute-start(f32[8,128]{1,0:T(8,128)} %bitcast.30), channel_id=1, source_target_pairs={{8,16},{16,8},{24,32},{32,24},{40,48},{48,40},{56,64},{64,56},{72,... | collective-permute-start | bytes 12296 | tf_op jit(solution)/shard_map/ppermute | solution.py:33
  1.3 8.5 %collective-permute-start = (f32[8,128]{1,0:T(8,128)}, f32[8,128]{1,0:T(8,128)S(1)}, u32[]{:S(2)}, u32[]{:S(2)}) collective-permute-start(f32[8,128]{1,0:T(8,128)} %bitcast.31), channel_id=1, source_target_pairs={{0,8},{8,0},{16,24},{24,16},{32,40},{40,32},{48,56},{56,48},{64,72... | collective-permute-start | bytes 12296 | tf_op jit(solution)/shard_map/ppermute | solution.py:33
  8.7 0.7 copy-start.4
  9.4 0.7 copy-start.3
  10.1 14.5 %copy-start.2 = (f32[1,1,8,128]{3,2,1,0:T(8,128)S(1)}, f32[1,1,8,128]{3,2,1,0:T(8,128)}, u32[]{:S(2)}) copy-start(f32[1,1,8,128]{3,2,1,0:T(8,128)} %param.9) | copy-start | bytes 12292
  10.1 13.7 %collective-permute-start.3 = (f32[3,8,128]{2,1,0:T(8,128)S(1)}, f32[3,8,128]{2,1,0:T(8,128)S(1)}, u32[]{:S(2)}, u32[]{:S(2)}) collective-permute-start(f32[3,8,128]{2,1,0:T(8,128)S(1)} %pad_maximum_fusion.refs_1_), channel_id=1, source_target_pairs={{1,2},{2,1},{3,4},{4,3},{5,6},{6,5},{9,10},{10,9},{11,12},{12,11},... | collective-permute-start | bytes 36872 | tf_op jit(solution)/shard_map/ppermute | solution.py:39
  14.6 10.0 %collective-permute-start.2 = (f32[3,8,128]{2,1,0:T(8,128)S(1)}, f32[3,8,128]{2,1,0:T(8,128)S(1)}, u32[]{:S(2)}, u32[]{:S(2)}) collective-permute-start(f32[3,8,128]{2,1,0:T(8,128)S(1)} %pad_maximum_fusion.refs_1_), channel_id=1, source_target_pairs={{0,1},{1,0},{2,3},{3,2},{4,5},{5,4},{6,7},{7,6},{8,9},{9,8},{10,11... | collective-permute-start | bytes 36872 | tf_op jit(solution)/shard_map/ppermute | solution.py:38
  24.6 1.2 copy-start
  25.8 11.0 %copy-start.1 = (bf16[1,1,8,4,128,128]{5,4,3,2,1,0:T(8,128)(2,1)S(1)}, bf16[1,1,8,4,128,128]{5,4,3,2,1,0:T(8,128)(2,1)}, u32[]{:S(2)}) copy-start(bf16[1,1,8,4,128,128]{5,4,3,2,1,0:T(8,128)(2,1)} %param.6) | copy-start | bytes 3145732
  26.7 3.6 %collective-permute-start.5 = (f32[8,128]{1,0:T(8,128)S(1)}, f32[8,128]{1,0:T(8,128)S(1)}, u32[]{:S(2)}, u32[]{:S(2)}) collective-permute-start(f32[8,128]{1,0:T(8,128)S(1)} %shard_map.68.u1), channel_id=1, source_target_pairs={{8,16},{16,8},{24,32},{32,24},{40,48},{48,40},{56,64},{64,56},{72,... | collective-permute-start | bytes 12296 | tf_op jit(solution)/shard_map/ppermute | solution.py:33
  27.4 4.4 %collective-permute-start.4 = (f32[8,128]{1,0:T(8,128)S(1)}, f32[8,128]{1,0:T(8,128)S(1)}, u32[]{:S(2)}, u32[]{:S(2)}) collective-permute-start(f32[8,128]{1,0:T(8,128)S(1)} %shard_map.68.u1), channel_id=1, source_target_pairs={{0,8},{8,0},{16,24},{24,16},{32,40},{40,32},{48,56},{56,48},{64,72... | collective-permute-start | bytes 12296 | tf_op jit(solution)/shard_map/ppermute | solution.py:33
  31.8 5.0 %collective-permute-start.7 = (f32[3,8,128]{2,1,0:T(8,128)S(1)}, f32[3,8,128]{2,1,0:T(8,128)S(1)}, u32[]{:S(2)}, u32[]{:S(2)}) collective-permute-start(f32[3,8,128]{2,1,0:T(8,128)S(1)} %pad_maximum_fusion.1.refs_1_), channel_id=1, source_target_pairs={{1,2},{2,1},{3,4},{4,3},{5,6},{6,5},{9,10},{10,9},{11,12},{12,11},... | collective-permute-start | bytes 36872 | tf_op jit(solution)/shard_map/ppermute | solution.py:39
  33.7 3.1 %collective-permute-start.6 = (f32[3,8,128]{2,1,0:T(8,128)S(1)}, f32[3,8,128]{2,1,0:T(8,128)S(1)}, u32[]{:S(2)}, u32[]{:S(2)}) collective-permute-start(f32[3,8,128]{2,1,0:T(8,128)S(1)} %pad_maximum_fusion.1.refs_1_), channel_id=1, source_target_pairs={{0,1},{1,0},{2,3},{3,2},{4,5},{5,4},{6,7},{7,6},{8,9},{9,8},{10,11... | collective-permute-start | bytes 36872 | tf_op jit(solution)/shard_map/ppermute | solution.py:38
  37.7 6.9 %collective-permute-start.9 = (f32[8,128]{1,0:T(8,128)S(1)}, f32[8,128]{1,0:T(8,128)S(1)}, u32[]{:S(2)}, u32[]{:S(2)}) collective-permute-start(f32[8,128]{1,0:T(8,128)S(1)} %shard_map.69.u2), channel_id=1, source_target_pairs={{8,16},{16,8},{24,32},{32,24},{40,48},{48,40},{56,64},{64,56},{72,... | collective-permute-start | bytes 12296 | tf_op jit(solution)/shard_map/ppermute | solution.py:33
  38.4 7.2 %collective-permute-start.8 = (f32[8,128]{1,0:T(8,128)S(1)}, f32[8,128]{1,0:T(8,128)S(1)}, u32[]{:S(2)}, u32[]{:S(2)}) collective-permute-start(f32[8,128]{1,0:T(8,128)S(1)} %shard_map.69.u2), channel_id=1, source_target_pairs={{0,8},{8,0},{16,24},{24,16},{32,40},{40,32},{48,56},{56,48},{64,72... | collective-permute-start | bytes 12296 | tf_op jit(solution)/shard_map/ppermute | solution.py:33
  45.6 6.1 %collective-permute-start.11 = (f32[3,8,128]{2,1,0:T(8,128)S(1)}, f32[3,8,128]{2,1,0:T(8,128)S(1)}, u32[]{:S(2)}, u32[]{:S(2)}) collective-permute-start(f32[3,8,128]{2,1,0:T(8,128)S(1)} %pad_maximum_fusion.2.refs_1_), channel_id=1, source_target_pairs={{1,2},{2,1},{3,4},{4,3},{5,6},{6,5},{9,10},{10,9},{11,12},{12,11},... | collective-permute-start | bytes 36872 | tf_op jit(solution)/shard_map/ppermute | solution.py:39
  49.7 3.1 %collective-permute-start.10 = (f32[3,8,128]{2,1,0:T(8,128)S(1)}, f32[3,8,128]{2,1,0:T(8,128)S(1)}, u32[]{:S(2)}, u32[]{:S(2)}) collective-permute-start(f32[3,8,128]{2,1,0:T(8,128)S(1)} %pad_maximum_fusion.2.refs_1_), channel_id=1, source_target_pairs={{0,1},{1,0},{2,3},{3,2},{4,5},{5,4},{6,7},{7,6},{8,9},{9,8},{10,11... | collective-permute-start | bytes 36872 | tf_op jit(solution)/shard_map/ppermute | solution.py:38
  53.7 8.2 %collective-permute-start.13 = (f32[8,128]{1,0:T(8,128)S(1)}, f32[8,128]{1,0:T(8,128)S(1)}, u32[]{:S(2)}, u32[]{:S(2)}) collective-permute-start(f32[8,128]{1,0:T(8,128)S(1)} %shard_map.70.u3), channel_id=1, source_target_pairs={{8,16},{16,8},{24,32},{32,24},{40,48},{48,40},{56,64},{64,56},{72,... | collective-permute-start | bytes 12296 | tf_op jit(solution)/shard_map/ppermute | solution.py:33
  54.4 8.5 %collective-permute-start.12 = (f32[8,128]{1,0:T(8,128)S(1)}, f32[8,128]{1,0:T(8,128)S(1)}, u32[]{:S(2)}, u32[]{:S(2)}) collective-permute-start(f32[8,128]{1,0:T(8,128)S(1)} %shard_map.70.u3), channel_id=1, source_target_pairs={{0,8},{8,0},{16,24},{24,16},{32,40},{40,32},{48,56},{56,48},{64,72... | collective-permute-start | bytes 12296 | tf_op jit(solution)/shard_map/ppermute | solution.py:33
  62.9 5.0 %collective-permute-start.15 = (f32[3,8,128]{2,1,0:T(8,128)S(1)}, f32[3,8,128]{2,1,0:T(8,128)S(1)}, u32[]{:S(2)}, u32[]{:S(2)}) collective-permute-start(f32[3,8,128]{2,1,0:T(8,128)S(1)} %pad_maximum_fusion.3.own), channel_id=1, source_target_pairs={{1,2},{2,1},{3,4},{4,3},{5,6},{6,5},{9,10},{10,9},{11,12},{12,11},... | collective-permute-start | bytes 36872 | tf_op jit(solution)/shard_map/ppermute | solution.py:39
  66.0 3.1 %collective-permute-start.14 = (f32[3,8,128]{2,1,0:T(8,128)S(1)}, f32[3,8,128]{2,1,0:T(8,128)S(1)}, u32[]{:S(2)}, u32[]{:S(2)}) collective-permute-start(f32[3,8,128]{2,1,0:T(8,128)S(1)} %pad_maximum_fusion.3.own), channel_id=1, source_target_pairs={{0,1},{1,0},{2,3},{3,2},{4,5},{5,4},{6,7},{7,6},{8,9},{9,8},{10,11... | collective-permute-start | bytes 36872 | tf_op jit(solution)/shard_map/ppermute | solution.py:38

commit v3 on v2

--- a/solution.py
+++ b/solution.py
@@ -28,56 +28,54 @@
 
 
 def exchange(field, rows, cols):
+    even, odd = swaps(cols)
+    beside = jnp.stack(
+        [field, lax.ppermute(field, COL, even), lax.ppermute(field, COL, odd)]
+    )
     even, odd = swaps(rows)
-    beside = jnp.stack(
-        [field, lax.ppermute(field, ROW, even), lax.ppermute(field, ROW, odd)]
-    )
-    even, odd = swaps(cols)
     return (
         beside,
-        lax.ppermute(beside, COL, even),
-        lax.ppermute(beside, COL, odd),
-    )
-
-
-def fill(halo, parts):
-    for at, part in enumerate(parts):
-        for row in range(3):
-            halo[pl.ds((at * 3 + row) * NB, NB), :] = part[row]
-    halo[pl.ds(9 * NB, NB), :] = jnp.zeros((NB, BS), F32)
-
-
-def multiply(index, halo, values, fine):
+        lax.ppermute(beside, ROW, even),
+        lax.ppermute(beside, ROW, odd),
+    )
+
+
+def multiply(pick, parts, values, fine):
+    halo = jnp.concatenate([part[...].reshape(3 * NB, BS) for part in parts], axis=0)
+    high = halo.astype(BF16).astype(F32)
+    halo = jnp.concatenate([high, halo - high], axis=1) if fine else high
+    taken = jnp.dot(pick[...], halo.astype(BF16), preferred_element_type=F32)
     sublane = lax.broadcasted_iota(jnp.int32, (NB, BS), 0)
     total = jnp.zeros((2 * NB, BS), F32)
     for n in range(NB):
-        pieces = []
+        left = []
         for s in range(SLOTS):
-            row = halo[pl.ds(index[n * SLOTS + s], 1), :]
-            row = jnp.where(sublane == n, jnp.broadcast_to(row, (NB, BS)), 0.0)
-            high = row.astype(BF16).astype(F32)
-            low = row - high if fine else jnp.zeros_like(row)
-            pieces.append(jnp.concatenate([high, low], axis=0).astype(BF16))
-        left = jnp.concatenate(pieces, axis=1)
+            rows = [taken[s * NB : (s + 1) * NB, at : at + BS] for at in range(0, taken.shape[1], BS)]
+            rows = [jnp.where(sublane == n, row, 0.0) for row in rows]
+            rows += [jnp.zeros_like(rows[0])] * (2 - len(rows))
+            left.append(jnp.concatenate(rows, axis=0).astype(BF16))
         right = jnp.concatenate([values[n * SLOTS + s] for s in range(SLOTS)], axis=1)
         total = total + lax.dot_general(
-            left, right, (((1,), (1,)), ((), ())), preferred_element_type=F32
+            jnp.concatenate(left, axis=1),
+            right,
+            (((1,), (1,)), ((), ())),
+            preferred_element_type=F32,
         )
     return total[:NB] + total[NB:]
 
 
-def apply_kernel(fine, index, own, even, odd, values, scale, out, halo):
-    fill(halo, (own, even, odd))
+def image(pick, own, even, odd, values, scale, fine):
     field = own[0]
-    product = multiply(index, halo, values, fine)
-    out[...] = (scale[...] * field - SHIFT * field) + product
-
-
-def last_kernel(index, own, even, odd, values, scale, u0, u1, u2, out, halo):
-    fill(halo, (own, even, odd))
-    field = own[0]
-    product = multiply(index, halo, values, True)
-    u4 = (scale[...] * field - SHIFT * field) + product
+    product = multiply(pick, (own, even, odd), values, fine)
+    return field, (scale[...] * field - SHIFT * field) + product
+
+
+def apply_kernel(fine, pick, own, even, odd, values, scale, out):
+    out[...] = image(pick, own, even, odd, values, scale, fine)[1]
+
+
+def last_kernel(pick, own, even, odd, values, scale, u0, u1, u2, out):
+    field, u4 = image(pick, own, even, odd, values, scale, True)
     fields = (u0[...], u1[...], u2[...], field, u4)
     lane = lax.broadcasted_iota(jnp.int32, (1, BS), 1)
     dots = jnp.zeros((1, BS), F32)
@@ -92,6 +90,12 @@
     total = jnp.sum(parts[...], axis=0)
     for at in range(out.shape[0]):
         out[at] = total
+
+
+def fetch_kernel(source, out, arrived):
+    copy = pltpu.make_async_copy(source, out, arrived)
+    copy.start()
+    copy.wait()
 
 
 def cholesky(gram, size):
@@ -165,15 +169,14 @@
     hessenberg[...] = matrix[:ITERS, :size]
 
 
-SMEM = pl.BlockSpec(memory_space=pltpu.SMEM)
 VMEM = pl.BlockSpec(memory_space=pltpu.VMEM)
 PARAMS = pltpu.CompilerParams(vmem_limit_bytes=4 << 20)
 FIELD = jax.ShapeDtypeStruct((NB, BS), F32)
 
 
-def halo_index(block_columns, live_slots):
-    where = block_columns.reshape(NB, SLOTS)
-    live = lax.broadcasted_iota(jnp.int32, (NB, SLOTS), 1) < live_slots.reshape(NB, 1)
+def slot_picks(block_columns, live_slots):
+    where = block_columns.reshape(NB, SLOTS).T
+    live = lax.broadcasted_iota(jnp.int32, (SLOTS, NB), 0) < live_slots.reshape(1, NB)
 
     def side(offset, position):
         forward = jnp.where(position % 2 == 0, 1, 2)
@@ -181,25 +184,33 @@
 
     row = side(where // (3 * NB), lax.axis_index(ROW))
     col = side(where // NB % 3, lax.axis_index(COL))
-    return jnp.where(live, (col * 3 + row) * NB + where % NB, 9 * NB).reshape(-1)
+    place = jnp.where(live, (row * 3 + col) * NB + where % NB, -1)
+    blocks = lax.broadcasted_iota(jnp.int32, (SLOTS, NB, 9 * NB), 2)
+    return (place[:, :, None] == blocks).astype(BF16).reshape(SLOTS * NB, 9 * NB)
 
 
 def on_device(rows, cols, right_side, block_values, block_columns, live_slots, row_scale):
     u0 = right_side.reshape(NB, BS)
     values = block_values.reshape(NB * SLOTS, BS, BS)
+    values = pl.pallas_call(
+        fetch_kernel,
+        out_shape=jax.ShapeDtypeStruct(values.shape, BF16),
+        in_specs=[pl.BlockSpec(memory_space=pltpu.HBM)],
+        out_specs=VMEM,
+        scratch_shapes=[pltpu.SemaphoreType.DMA],
+        compiler_params=pltpu.CompilerParams(vmem_limit_bytes=52 << 20),
+    )(values)
     scale = row_scale.reshape(NB, BS)
-    index = halo_index(block_columns, live_slots)
-    halo = [pltpu.VMEM((10 * NB, BS), F32)]
+    pick = slot_picks(block_columns, live_slots)
 
     def apply(field, fine):
         return pl.pallas_call(
             lambda *refs: apply_kernel(fine, *refs),
             out_shape=FIELD,
-            in_specs=[SMEM] + [VMEM] * 5,
+            in_specs=[VMEM] * 6,
             out_specs=VMEM,
-            scratch_shapes=halo,
             compiler_params=PARAMS,
-        )(index, *exchange(field, rows, cols), values, scale)
+        )(pick, *exchange(field, rows, cols), values, scale)
 
     u1 = apply(u0, False)
     u2 = apply(u1, True)
@@ -209,11 +220,10 @@
     parts = pl.pallas_call(
         last_kernel,
         out_shape=jax.ShapeDtypeStruct((plane, 1, BS), F32),
-        in_specs=[SMEM] + [VMEM] * 8,
+        in_specs=[VMEM] * 9,
         out_specs=VMEM,
-        scratch_shapes=halo,
         compiler_params=PARAMS,
-    )(index, *exchange(u3, rows, cols), values, scale, u0, u1, u2)
+    )(pick, *exchange(u3, rows, cols), values, scale, u0, u1, u2)
     parts = lax.all_to_all(parts, PLANE, split_axis=0, concat_axis=0, tiled=True)
     parts = pl.pallas_call(
         sum_kernel,

time: 130 us -> 127 us (0.977)
  starting transfers between devices: 55.3 us -> 53.3 us
    ppermute x16, starting transfers between devices: 55.3 us -> 53.3 us  [the longest x4 18.5 us: exchange(): lax.ppermute(beside, ROW, even)]
    pallas_call x3, Pallas kernels: 2.73 us -> 1.39 us  [apply(): pl.pallas_call(lambda *refs: apply_kernel(fine, *refs), out_shape=FIELD,...]
  transfers between devices with their start and end apart: 16 -> 16, of which waited for: 8 -> 9; matrix products, arithmetic and copies ran while one was open for 0% -> 0% of each run, Pallas kernels for 0% -> 1%
where the time goes in v3:
time: 127 us
  blocking collectives  59.3 us (47%)
  starting transfers between devices  53.3 us (42%)
  waiting for transfers between devices  7.91 us (6%)
  Pallas kernels  4.13 us (3%)
    all_to_all x1, blocking collectives, on_device(): parts = lax.all_to_all(parts, 'z', split_axis=0, concat_axis=0, tiled=True)  34.5 us
    all_to_all x1, blocking collectives, on_device(): lax.all_to_all(parts, PLANE, split_axis=0, concat_axis=0, tiled=True)  24.7 us
    ppermute x4, starting transfers between devices, exchange(): lax.ppermute(beside, ROW, even)  18.5 us
    ppermute x4, starting transfers between devices, exchange(): lax.ppermute(field, COL, even)  18 us
    ppermute x4, starting transfers between devices, exchange(): lax.ppermute(field, COL, odd)  14.2 us
    ppermute x4, waiting for transfers between devices, exchange(): lax.ppermute(beside, ROW, even)  4.35 us
    ppermute x4, starting transfers between devices, exchange(): lax.ppermute(beside, ROW, odd)  2.6 us
  transfers between devices with their start and end apart: 16, of which 9 were waited for; matrix products, arithmetic and copies ran while one was open for 0% of the time, Pallas kernels for 1%

profile of v3, /device:TPU:1, one launch (start us, length us, event | category | flops | bytes accessed | tf_op | source)
XLA Modules:
  0.0 126.8 jit_solution(1595810251544392)
XLA Ops:
  0.6 4.5 %collective-permute-start.1 = (f32[8,128]{1,0:T(8,128)}, f32[8,128]{1,0:T(8,128)S(1)}, u32[]{:S(2)}, u32[]{:S(2)}) collective-permute-start(f32[8,128]{1,0:T(8,128)} %bitcast.48), channel_id=1, source_target_pairs={{1,2},{2,1},{3,4},{4,3},{5,6},{6,5},{9,10},{10,9},{11,12},{12,11},... | collective-permute-start | bytes 12296 | tf_op jit(solution)/shard_map/ppermute | solution.py:33
  5.1 12.2 %collective-permute-start = (f32[8,128]{1,0:T(8,128)}, f32[8,128]{1,0:T(8,128)S(1)}, u32[]{:S(2)}, u32[]{:S(2)}) collective-permute-start(f32[8,128]{1,0:T(8,128)} %bitcast.49), channel_id=1, source_target_pairs={{0,1},{1,0},{2,3},{3,2},{4,5},{5,4},{6,7},{7,6},{8,9},{9,8},{10,11... | collective-permute-start | bytes 12296 | tf_op jit(solution)/shard_map/ppermute | solution.py:33
  17.4 0.0 copy-start.2
  17.4 0.0 copy-start.3
  17.4 0.7 copy-done.2
  18.1 0.0 copy-done.3
  18.1 0.0 copy-start.1
  18.1 0.1 eq.41
  18.2 0.0 collective-permute-done.1
  18.2 0.2 collective-permute-done
  18.4 0.4 copy-done.1
  18.8 0.7 collective-permute-start.3
  19.5 1.9 %collective-permute-start.2 = (f32[3,8,128]{2,1,0:T(8,128)S(1)}, f32[3,8,128]{2,1,0:T(8,128)S(1)}, u32[]{:S(2)}, u32[]{:S(2)}) collective-permute-start(f32[3,8,128]{2,1,0:T(8,128)S(1)} %pad_maximum_fusion.refs_1_), channel_id=1, source_target_pairs={{0,8},{8,0},{16,24},{24,16},{32,40},{40,32},{48,56},{56,48},{64,72... | collective-permute-start | bytes 36872 | tf_op jit(solution)/shard_map/ppermute | solution.py:38
  21.4 0.1 fusion.refs_0_.pick
  21.5 0.0 copy-start
  21.5 1.2 shard_map.68.refs_4_.values
  22.7 0.0 collective-permute-done.3.refs_3_
  22.7 1.2 collective-permute-done.2.refs_2_
  23.9 0.0 copy-done
  23.9 0.5 shard_map.69.u1
  24.4 1.9 %collective-permute-start.5 = (f32[8,128]{1,0:T(8,128)S(1)}, f32[8,128]{1,0:T(8,128)S(1)}, u32[]{:S(2)}, u32[]{:S(2)}) collective-permute-start(f32[8,128]{1,0:T(8,128)S(1)} %shard_map.69.u1), channel_id=1, source_target_pairs={{1,2},{2,1},{3,4},{4,3},{5,6},{6,5},{9,10},{10,9},{11,12},{12,11},... | collective-permute-start | bytes 12296 | tf_op jit(solution)/shard_map/ppermute | solution.py:33
  26.3 1.9 %collective-permute-start.4 = (f32[8,128]{1,0:T(8,128)S(1)}, f32[8,128]{1,0:T(8,128)S(1)}, u32[]{:S(2)}, u32[]{:S(2)}) collective-permute-start(f32[8,128]{1,0:T(8,128)S(1)} %shard_map.69.u1), channel_id=1, source_target_pairs={{0,1},{1,0},{2,3},{3,2},{4,5},{5,4},{6,7},{7,6},{8,9},{9,8},{10,11... | collective-permute-start | bytes 12296 | tf_op jit(solution)/shard_map/ppermute | solution.py:33
  28.2 1.1 collective-permute-done.5
  29.3 0.1 collective-permute-done.4
  29.4 0.7 collective-permute-start.7
  30.0 3.5 %collective-permute-start.6 = (f32[3,8,128]{2,1,0:T(8,128)S(1)}, f32[3,8,128]{2,1,0:T(8,128)S(1)}, u32[]{:S(2)}, u32[]{:S(2)}) collective-permute-start(f32[3,8,128]{2,1,0:T(8,128)S(1)} %pad_maximum_fusion.1.refs_1_), channel_id=1, source_target_pairs={{0,8},{8,0},{16,24},{24,16},{32,40},{40,32},{48,56},{56,48},{64,72... | collective-permute-start | bytes 36872 | tf_op jit(solution)/shard_map/ppermute | solution.py:38
  33.5 0.0 collective-permute-done.7.refs_3_
  33.5 1.1 collective-permute-done.6.refs_2_
  34.6 0.5 shard_map.70.u2
  35.0 4.7 %collective-permute-start.9 = (f32[8,128]{1,0:T(8,128)S(1)}, f32[8,128]{1,0:T(8,128)S(1)}, u32[]{:S(2)}, u32[]{:S(2)}) collective-permute-start(f32[8,128]{1,0:T(8,128)S(1)} %shard_map.70.u2), channel_id=1, source_target_pairs={{1,2},{2,1},{3,4},{4,3},{5,6},{6,5},{9,10},{10,9},{11,12},{12,11},... | collective-permute-start | bytes 12296 | tf_op jit(solution)/shard_map/ppermute | solution.py:33
  39.7 1.9 %collective-permute-start.8 = (f32[8,128]{1,0:T(8,128)S(1)}, f32[8,128]{1,0:T(8,128)S(1)}, u32[]{:S(2)}, u32[]{:S(2)}) collective-permute-start(f32[8,128]{1,0:T(8,128)S(1)} %shard_map.70.u2), channel_id=1, source_target_pairs={{0,1},{1,0},{2,3},{3,2},{4,5},{5,4},{6,7},{7,6},{8,9},{9,8},{10,11... | collective-permute-start | bytes 12296 | tf_op jit(solution)/shard_map/ppermute | solution.py:33
  41.7 0.0 collective-permute-done.9
  41.7 1.1 collective-permute-done.8
  42.8 0.7 collective-permute-start.11
  43.5 6.5 %collective-permute-start.10 = (f32[3,8,128]{2,1,0:T(8,128)S(1)}, f32[3,8,128]{2,1,0:T(8,128)S(1)}, u32[]{:S(2)}, u32[]{:S(2)}) collective-permute-start(f32[3,8,128]{2,1,0:T(8,128)S(1)} %pad_maximum_fusion.2.refs_1_), channel_id=1, source_target_pairs={{0,8},{8,0},{16,24},{24,16},{32,40},{40,32},{48,56},{56,48},{64,72... | collective-permute-start | bytes 36872 | tf_op jit(solution)/shard_map/ppermute | solution.py:38
  49.9 0.0 collective-permute-done.11.refs_3_
  49.9 1.1 collective-permute-done.10.refs_2_
  51.0 0.5 shard_map.71.u3
  51.5 3.1 %collective-permute-start.13 = (f32[8,128]{1,0:T(8,128)S(1)}, f32[8,128]{1,0:T(8,128)S(1)}, u32[]{:S(2)}, u32[]{:S(2)}) collective-permute-start(f32[8,128]{1,0:T(8,128)S(1)} %shard_map.71.u3), channel_id=1, source_target_pairs={{1,2},{2,1},{3,4},{4,3},{5,6},{6,5},{9,10},{10,9},{11,12},{12,11},... | collective-permute-start | bytes 12296 | tf_op jit(solution)/shard_map/ppermute | solution.py:33
  54.6 1.9 %collective-permute-start.12 = (f32[8,128]{1,0:T(8,128)S(1)}, f32[8,128]{1,0:T(8,128)S(1)}, u32[]{:S(2)}, u32[]{:S(2)}) collective-permute-start(f32[8,128]{1,0:T(8,128)S(1)} %shard_map.71.u3), channel_id=1, source_target_pairs={{0,1},{1,0},{2,3},{3,2},{4,5},{5,4},{6,7},{7,6},{8,9},{9,8},{10,11... | collective-permute-start | bytes 12296 | tf_op jit(solution)/shard_map/ppermute | solution.py:33
  56.5 0.0 collective-permute-done.13
  56.5 1.1 collective-permute-done.12
  57.6 0.7 collective-permute-start.15
  58.3 6.6 %collective-permute-start.14 = (f32[3,8,128]{2,1,0:T(8,128)S(1)}, f32[3,8,128]{2,1,0:T(8,128)S(1)}, u32[]{:S(2)}, u32[]{:S(2)}) collective-permute-start(f32[3,8,128]{2,1,0:T(8,128)S(1)} %pad_maximum_fusion.3.own), channel_id=1, source_target_pairs={{0,8},{8,0},{16,24},{24,16},{32,40},{40,32},{48,56},{56,48},{64,72... | collective-permute-start | bytes 36872 | tf_op jit(solution)/shard_map/ppermute | solution.py:38
  64.9 0.0 collective-permute-done.15.odd
  64.9 1.1 collective-permute-done.14.even
  66.0 0.6 shard_map.72
  66.6 24.7 %all_to_all.10.parts = f32[32,1,128]{2,1,0:T(1,128)S(1)} all-to-all(f32[32,1,128]{2,1,0:T(1,128)S(1)} %shard_map.72), channel_id=1, replica_groups=mesh['y'=4,'z'=32,'x'=4,'core'=2] {'y','x','core'}, dimensions={0} | all-to-all | bytes 32768 | tf_op jit(solution)/shard_map/all_to_all | solution.py:227
  91.4 34.5 %all_to_all.11.parts = f32[32,1,128]{2,1,0:T(1,128)S(1)} all-to-all(f32[32,1,128]{2,1,0:T(1,128)S(1)} %shard_map.73), channel_id=1, replica_groups=mesh['y'=4,'z'=32,'x'=4,'core'=2] {'z'}, dimensions={0} | all-to-all | bytes 32768 | tf_op jit(solution)/shard_map/all_to_all | solution.py:235
  125.9 0.8 shard_map.74
  (6 shorter events, 0.1 us)
Async XLA Ops:
  0.6 17.6 %collective-permute-start.1 = (f32[8,128]{1,0:T(8,128)}, f32[8,128]{1,0:T(8,128)S(1)}, u32[]{:S(2)}, u32[]{:S(2)}) collective-permute-start(f32[8,128]{1,0:T(8,128)} %bitcast.48), channel_id=1, source_target_pairs={{1,2},{2,1},{3,4},{4,3},{5,6},{6,5},{9,10},{10,9},{11,12},{12,11},... | collective-permute-start | bytes 12296 | tf_op jit(solution)/shard_map/ppermute | solution.py:33
  5.1 13.2 %collective-permute-start = (f32[8,128]{1,0:T(8,128)}, f32[8,128]{1,0:T(8,128)S(1)}, u32[]{:S(2)}, u32[]{:S(2)}) collective-permute-start(f32[8,128]{1,0:T(8,128)} %bitcast.49), channel_id=1, source_target_pairs={{0,1},{1,0},{2,3},{3,2},{4,5},{5,4},{6,7},{7,6},{8,9},{9,8},{10,11... | collective-permute-start | bytes 12296 | tf_op jit(solution)/shard_map/ppermute | solution.py:33
  17.4 0.7 copy-start.2
  17.4 0.7 copy-start.3
  18.1 0.7 copy-start.1
  18.8 3.9 %collective-permute-start.3 = (f32[3,8,128]{2,1,0:T(8,128)S(1)}, f32[3,8,128]{2,1,0:T(8,128)S(1)}, u32[]{:S(2)}, u32[]{:S(2)}) collective-permute-start(f32[3,8,128]{2,1,0:T(8,128)S(1)} %pad_maximum_fusion.refs_1_), channel_id=1, source_target_pairs={{8,16},{16,8},{24,32},{32,24},{40,48},{48,40},{56,64},{64,56},{72,... | collective-permute-start | bytes 36872 | tf_op jit(solution)/shard_map/ppermute | solution.py:39
  19.5 4.4 %collective-permute-start.2 = (f32[3,8,128]{2,1,0:T(8,128)S(1)}, f32[3,8,128]{2,1,0:T(8,128)S(1)}, u32[]{:S(2)}, u32[]{:S(2)}) collective-permute-start(f32[3,8,128]{2,1,0:T(8,128)S(1)} %pad_maximum_fusion.refs_1_), channel_id=1, source_target_pairs={{0,8},{8,0},{16,24},{24,16},{32,40},{40,32},{48,56},{56,48},{64,72... | collective-permute-start | bytes 36872 | tf_op jit(solution)/shard_map/ppermute | solution.py:38
  21.5 2.4 %copy-start = (f32[1,1,8,128]{3,2,1,0:T(8,128)S(1)}, f32[1,1,8,128]{3,2,1,0:T(8,128)}, u32[]{:S(2)}) copy-start(f32[1,1,8,128]{3,2,1,0:T(8,128)} %param.9) | copy-start | bytes 12292
  24.4 4.9 %collective-permute-start.5 = (f32[8,128]{1,0:T(8,128)S(1)}, f32[8,128]{1,0:T(8,128)S(1)}, u32[]{:S(2)}, u32[]{:S(2)}) collective-permute-start(f32[8,128]{1,0:T(8,128)S(1)} %shard_map.69.u1), channel_id=1, source_target_pairs={{1,2},{2,1},{3,4},{4,3},{5,6},{6,5},{9,10},{10,9},{11,12},{12,11},... | collective-permute-start | bytes 12296 | tf_op jit(solution)/shard_map/ppermute | solution.py:33
  26.3 3.1 %collective-permute-start.4 = (f32[8,128]{1,0:T(8,128)S(1)}, f32[8,128]{1,0:T(8,128)S(1)}, u32[]{:S(2)}, u32[]{:S(2)}) collective-permute-start(f32[8,128]{1,0:T(8,128)S(1)} %shard_map.69.u1), channel_id=1, source_target_pairs={{0,1},{1,0},{2,3},{3,2},{4,5},{5,4},{6,7},{7,6},{8,9},{9,8},{10,11... | collective-permute-start | bytes 12296 | tf_op jit(solution)/shard_map/ppermute | solution.py:33
  29.4 4.1 %collective-permute-start.7 = (f32[3,8,128]{2,1,0:T(8,128)S(1)}, f32[3,8,128]{2,1,0:T(8,128)S(1)}, u32[]{:S(2)}, u32[]{:S(2)}) collective-permute-start(f32[3,8,128]{2,1,0:T(8,128)S(1)} %pad_maximum_fusion.1.refs_1_), channel_id=1, source_target_pairs={{8,16},{16,8},{24,32},{32,24},{40,48},{48,40},{56,64},{64,56},{72,... | collective-permute-start | bytes 36872 | tf_op jit(solution)/shard_map/ppermute | solution.py:39
  30.0 4.5 %collective-permute-start.6 = (f32[3,8,128]{2,1,0:T(8,128)S(1)}, f32[3,8,128]{2,1,0:T(8,128)S(1)}, u32[]{:S(2)}, u32[]{:S(2)}) collective-permute-start(f32[3,8,128]{2,1,0:T(8,128)S(1)} %pad_maximum_fusion.1.refs_1_), channel_id=1, source_target_pairs={{0,8},{8,0},{16,24},{24,16},{32,40},{40,32},{48,56},{56,48},{64,72... | collective-permute-start | bytes 36872 | tf_op jit(solution)/shard_map/ppermute | solution.py:38
  35.0 6.6 %collective-permute-start.9 = (f32[8,128]{1,0:T(8,128)S(1)}, f32[8,128]{1,0:T(8,128)S(1)}, u32[]{:S(2)}, u32[]{:S(2)}) collective-permute-start(f32[8,128]{1,0:T(8,128)S(1)} %shard_map.70.u2), channel_id=1, source_target_pairs={{1,2},{2,1},{3,4},{4,3},{5,6},{6,5},{9,10},{10,9},{11,12},{12,11},... | collective-permute-start | bytes 12296 | tf_op jit(solution)/shard_map/ppermute | solution.py:33
  39.7 3.1 %collective-permute-start.8 = (f32[8,128]{1,0:T(8,128)S(1)}, f32[8,128]{1,0:T(8,128)S(1)}, u32[]{:S(2)}, u32[]{:S(2)}) collective-permute-start(f32[8,128]{1,0:T(8,128)S(1)} %shard_map.70.u2), channel_id=1, source_target_pairs={{0,1},{1,0},{2,3},{3,2},{4,5},{5,4},{6,7},{7,6},{8,9},{9,8},{10,11... | collective-permute-start | bytes 12296 | tf_op jit(solution)/shard_map/ppermute | solution.py:33
  42.8 7.1 %collective-permute-start.11 = (f32[3,8,128]{2,1,0:T(8,128)S(1)}, f32[3,8,128]{2,1,0:T(8,128)S(1)}, u32[]{:S(2)}, u32[]{:S(2)}) collective-permute-start(f32[3,8,128]{2,1,0:T(8,128)S(1)} %pad_maximum_fusion.2.refs_1_), channel_id=1, source_target_pairs={{8,16},{16,8},{24,32},{32,24},{40,48},{48,40},{56,64},{64,56},{72,... | collective-permute-start | bytes 36872 | tf_op jit(solution)/shard_map/ppermute | solution.py:39
  43.5 7.5 %collective-permute-start.10 = (f32[3,8,128]{2,1,0:T(8,128)S(1)}, f32[3,8,128]{2,1,0:T(8,128)S(1)}, u32[]{:S(2)}, u32[]{:S(2)}) collective-permute-start(f32[3,8,128]{2,1,0:T(8,128)S(1)} %pad_maximum_fusion.2.refs_1_), channel_id=1, source_target_pairs={{0,8},{8,0},{16,24},{24,16},{32,40},{40,32},{48,56},{56,48},{64,72... | collective-permute-start | bytes 36872 | tf_op jit(solution)/shard_map/ppermute | solution.py:38
  51.5 5.0 %collective-permute-start.13 = (f32[8,128]{1,0:T(8,128)S(1)}, f32[8,128]{1,0:T(8,128)S(1)}, u32[]{:S(2)}, u32[]{:S(2)}) collective-permute-start(f32[8,128]{1,0:T(8,128)S(1)} %shard_map.71.u3), channel_id=1, source_target_pairs={{1,2},{2,1},{3,4},{4,3},{5,6},{6,5},{9,10},{10,9},{11,12},{12,11},... | collective-permute-start | bytes 12296 | tf_op jit(solution)/shard_map/ppermute | solution.py:33
  54.6 3.1 %collective-permute-start.12 = (f32[8,128]{1,0:T(8,128)S(1)}, f32[8,128]{1,0:T(8,128)S(1)}, u32[]{:S(2)}, u32[]{:S(2)}) collective-permute-start(f32[8,128]{1,0:T(8,128)S(1)} %shard_map.71.u3), channel_id=1, source_target_pairs={{0,1},{1,0},{2,3},{3,2},{4,5},{5,4},{6,7},{7,6},{8,9},{9,8},{10,11... | collective-permute-start | bytes 12296 | tf_op jit(solution)/shard_map/ppermute | solution.py:33
  57.6 7.3 %collective-permute-start.15 = (f32[3,8,128]{2,1,0:T(8,128)S(1)}, f32[3,8,128]{2,1,0:T(8,128)S(1)}, u32[]{:S(2)}, u32[]{:S(2)}) collective-permute-start(f32[3,8,128]{2,1,0:T(8,128)S(1)} %pad_maximum_fusion.3.own), channel_id=1, source_target_pairs={{8,16},{16,8},{24,32},{32,24},{40,48},{48,40},{56,64},{64,56},{72,... | collective-permute-start | bytes 36872 | tf_op jit(solution)/shard_map/ppermute | solution.py:39
  58.3 7.7 %collective-permute-start.14 = (f32[3,8,128]{2,1,0:T(8,128)S(1)}, f32[3,8,128]{2,1,0:T(8,128)S(1)}, u32[]{:S(2)}, u32[]{:S(2)}) collective-permute-start(f32[3,8,128]{2,1,0:T(8,128)S(1)} %pad_maximum_fusion.3.own), channel_id=1, source_target_pairs={{0,8},{8,0},{16,24},{24,16},{32,40},{40,32},{48,56},{56,48},{64,72... | collective-permute-start | bytes 36872 | tf_op jit(solution)/shard_map/ppermute | solution.py:38

commit v4 on v3

--- a/solution.py
+++ b/solution.py
@@ -54,12 +54,9 @@
             rows = [jnp.where(sublane == n, row, 0.0) for row in rows]
             rows += [jnp.zeros_like(rows[0])] * (2 - len(rows))
             left.append(jnp.concatenate(rows, axis=0).astype(BF16))
-        right = jnp.concatenate([values[n * SLOTS + s] for s in range(SLOTS)], axis=1)
-        total = total + lax.dot_general(
-            jnp.concatenate(left, axis=1),
-            right,
-            (((1,), (1,)), ((), ())),
-            preferred_element_type=F32,
+        right = jnp.concatenate([values[n * SLOTS + s] for s in range(SLOTS)], axis=0)
+        total = total + jnp.dot(
+            jnp.concatenate(left, axis=1), right, preferred_element_type=F32
         )
     return total[:NB] + total[NB:]
 
@@ -92,10 +89,19 @@
         out[at] = total
 
 
-def fetch_kernel(source, out, arrived):
-    copy = pltpu.make_async_copy(source, out, arrived)
-    copy.start()
-    copy.wait()
+def fetch_kernel(source, out, landed, arrived):
+    copies = [
+        pltpu.make_async_copy(
+            source.at[pl.ds(n * SLOTS, SLOTS)], landed.at[pl.ds(n * SLOTS, SLOTS)], arrived.at[n]
+        )
+        for n in range(NB)
+    ]
+    for copy in copies:
+        copy.start()
+    for n in range(NB):
+        copies[n].wait()
+        for s in range(SLOTS):
+            out[n * SLOTS + s] = landed[n * SLOTS + s].T
 
 
 def cholesky(gram, size):
@@ -197,7 +203,10 @@
         out_shape=jax.ShapeDtypeStruct(values.shape, BF16),
         in_specs=[pl.BlockSpec(memory_space=pltpu.HBM)],
         out_specs=VMEM,
-        scratch_shapes=[pltpu.SemaphoreType.DMA],
+        scratch_shapes=[
+            pltpu.VMEM(values.shape, BF16),
+            pltpu.SemaphoreType.DMA((NB,)),
+        ],
         compiler_params=pltpu.CompilerParams(vmem_limit_bytes=52 << 20),
     )(values)
     scale = row_scale.reshape(NB, BS)

time: 127 us -> 127 us (level)
  no operation moved by 1% of the time
where the time goes in v4:
time: 127 us; the launch traced here: 126 us
  blocking collectives  59.1 us (47%)
  starting transfers between devices  53.4 us (42%)
  waiting for transfers between devices  7.46 us (6%)
  Pallas kernels  4.15 us (3%)
    all_to_all x1, blocking collectives, on_device(): parts = lax.all_to_all(parts, 'z', split_axis=0, concat_axis=0, tiled=True)  34.4 us
    all_to_all x1, blocking collectives, on_device(): lax.all_to_all(parts, PLANE, split_axis=0, concat_axis=0, tiled=True)  24.7 us
    ppermute x4, starting transfers between devices, exchange(): lax.ppermute(beside, ROW, even)  18.8 us
    ppermute x4, starting transfers between devices, exchange(): lax.ppermute(field, COL, even)  18 us
    ppermute x4, starting transfers between devices, exchange(): lax.ppermute(field, COL, odd)  14 us
    ppermute x4, waiting for transfers between devices, exchange(): lax.ppermute(beside, ROW, even)  3.89 us
    ppermute x4, starting transfers between devices, exchange(): lax.ppermute(beside, ROW, odd)  2.6 us
  transfers between devices with their start and end apart: 16, of which 9 were waited for; matrix products, arithmetic and copies ran while one was open for 0% of the time, Pallas kernels for 1%

profile of v4, /device:TPU:1, one launch (start us, length us, event | category | flops | bytes accessed | tf_op | source)
XLA Modules:
  0.0 126.3 jit_solution(15670871233425803570)
XLA Ops:
  0.6 4.5 %collective-permute-start.1 = (f32[8,128]{1,0:T(8,128)}, f32[8,128]{1,0:T(8,128)S(1)}, u32[]{:S(2)}, u32[]{:S(2)}) collective-permute-start(f32[8,128]{1,0:T(8,128)} %bitcast.48), channel_id=1, source_target_pairs={{1,2},{2,1},{3,4},{4,3},{5,6},{6,5},{9,10},{10,9},{11,12},{12,11},... | collective-permute-start | bytes 12296 | tf_op jit(solution)/shard_map/ppermute | solution.py:33
  5.1 12.2 %collective-permute-start = (f32[8,128]{1,0:T(8,128)}, f32[8,128]{1,0:T(8,128)S(1)}, u32[]{:S(2)}, u32[]{:S(2)}) collective-permute-start(f32[8,128]{1,0:T(8,128)} %bitcast.49), channel_id=1, source_target_pairs={{0,1},{1,0},{2,3},{3,2},{4,5},{5,4},{6,7},{7,6},{8,9},{9,8},{10,11... | collective-permute-start | bytes 12296 | tf_op jit(solution)/shard_map/ppermute | solution.py:33
  17.4 0.0 copy-start.2
  17.4 0.0 copy-start.3
  17.4 0.7 copy-done.2
  18.1 0.0 copy-done.3
  18.1 0.0 copy-start.1
  18.1 0.1 eq.41
  18.2 0.0 collective-permute-done.1
  18.2 0.2 collective-permute-done
  18.4 0.4 copy-done.1
  18.8 0.7 collective-permute-start.3
  19.5 1.9 %collective-permute-start.2 = (f32[3,8,128]{2,1,0:T(8,128)S(1)}, f32[3,8,128]{2,1,0:T(8,128)S(1)}, u32[]{:S(2)}, u32[]{:S(2)}) collective-permute-start(f32[3,8,128]{2,1,0:T(8,128)S(1)} %pad_maximum_fusion.refs_1_), channel_id=1, source_target_pairs={{0,8},{8,0},{16,24},{24,16},{32,40},{40,32},{48,56},{56,48},{64,72... | collective-permute-start | bytes 36872 | tf_op jit(solution)/shard_map/ppermute | solution.py:38
  21.4 0.1 fusion.refs_0_.pick
  21.5 0.0 copy-start
  21.5 1.7 %shard_map.68.refs_4_.values = bf16[32,128,128]{2,1,0:T(8,128)(2,1)S(1)} custom-call(bf16[32,128,128]{2,1,0:T(8,128)(2,1)} %bitcast.54), custom_call_target="tpu_custom_call" | custom-call | tf_op jit(solution)/shard_map/pallas_call | solution.py:201
  23.2 0.0 collective-permute-done.3.refs_3_
  23.2 0.7 collective-permute-done.2.refs_2_
  23.9 0.0 copy-done
  23.9 0.4 shard_map.69.u1
  24.3 1.9 %collective-permute-start.5 = (f32[8,128]{1,0:T(8,128)S(1)}, f32[8,128]{1,0:T(8,128)S(1)}, u32[]{:S(2)}, u32[]{:S(2)}) collective-permute-start(f32[8,128]{1,0:T(8,128)S(1)} %shard_map.69.u1), channel_id=1, source_target_pairs={{1,2},{2,1},{3,4},{4,3},{5,6},{6,5},{9,10},{10,9},{11,12},{12,11},... | collective-permute-start | bytes 12296 | tf_op jit(solution)/shard_map/ppermute | solution.py:33
  26.2 1.9 %collective-permute-start.4 = (f32[8,128]{1,0:T(8,128)S(1)}, f32[8,128]{1,0:T(8,128)S(1)}, u32[]{:S(2)}, u32[]{:S(2)}) collective-permute-start(f32[8,128]{1,0:T(8,128)S(1)} %shard_map.69.u1), channel_id=1, source_target_pairs={{0,1},{1,0},{2,3},{3,2},{4,5},{5,4},{6,7},{7,6},{8,9},{9,8},{10,11... | collective-permute-start | bytes 12296 | tf_op jit(solution)/shard_map/ppermute | solution.py:33
  28.1 1.1 collective-permute-done.5
  29.2 0.1 collective-permute-done.4
  29.3 0.7 collective-permute-start.7
  29.9 3.9 %collective-permute-start.6 = (f32[3,8,128]{2,1,0:T(8,128)S(1)}, f32[3,8,128]{2,1,0:T(8,128)S(1)}, u32[]{:S(2)}, u32[]{:S(2)}) collective-permute-start(f32[3,8,128]{2,1,0:T(8,128)S(1)} %pad_maximum_fusion.1.refs_1_), channel_id=1, source_target_pairs={{0,8},{8,0},{16,24},{24,16},{32,40},{40,32},{48,56},{56,48},{64,72... | collective-permute-start | bytes 36872 | tf_op jit(solution)/shard_map/ppermute | solution.py:38
  33.8 0.0 collective-permute-done.7.refs_3_
  33.9 1.1 collective-permute-done.6.refs_2_
  34.9 0.4 shard_map.70.u2
  35.3 4.5 %collective-permute-start.9 = (f32[8,128]{1,0:T(8,128)S(1)}, f32[8,128]{1,0:T(8,128)S(1)}, u32[]{:S(2)}, u32[]{:S(2)}) collective-permute-start(f32[8,128]{1,0:T(8,128)S(1)} %shard_map.70.u2), channel_id=1, source_target_pairs={{1,2},{2,1},{3,4},{4,3},{5,6},{6,5},{9,10},{10,9},{11,12},{12,11},... | collective-permute-start | bytes 12296 | tf_op jit(solution)/shard_map/ppermute | solution.py:33
  39.8 1.9 %collective-permute-start.8 = (f32[8,128]{1,0:T(8,128)S(1)}, f32[8,128]{1,0:T(8,128)S(1)}, u32[]{:S(2)}, u32[]{:S(2)}) collective-permute-start(f32[8,128]{1,0:T(8,128)S(1)} %shard_map.70.u2), channel_id=1, source_target_pairs={{0,1},{1,0},{2,3},{3,2},{4,5},{5,4},{6,7},{7,6},{8,9},{9,8},{10,11... | collective-permute-start | bytes 12296 | tf_op jit(solution)/shard_map/ppermute | solution.py:33
  41.7 0.0 collective-permute-done.9
  41.7 1.1 collective-permute-done.8
  42.9 0.7 collective-permute-start.11
  43.5 6.6 %collective-permute-start.10 = (f32[3,8,128]{2,1,0:T(8,128)S(1)}, f32[3,8,128]{2,1,0:T(8,128)S(1)}, u32[]{:S(2)}, u32[]{:S(2)}) collective-permute-start(f32[3,8,128]{2,1,0:T(8,128)S(1)} %pad_maximum_fusion.2.refs_1_), channel_id=1, source_target_pairs={{0,8},{8,0},{16,24},{24,16},{32,40},{40,32},{48,56},{56,48},{64,72... | collective-permute-start | bytes 36872 | tf_op jit(solution)/shard_map/ppermute | solution.py:38
  50.2 0.0 collective-permute-done.11.refs_3_
  50.2 1.1 collective-permute-done.10.refs_2_
  51.2 0.4 shard_map.71.u3
  51.6 3.1 %collective-permute-start.13 = (f32[8,128]{1,0:T(8,128)S(1)}, f32[8,128]{1,0:T(8,128)S(1)}, u32[]{:S(2)}, u32[]{:S(2)}) collective-permute-start(f32[8,128]{1,0:T(8,128)S(1)} %shard_map.71.u3), channel_id=1, source_target_pairs={{1,2},{2,1},{3,4},{4,3},{5,6},{6,5},{9,10},{10,9},{11,12},{12,11},... | collective-permute-start | bytes 12296 | tf_op jit(solution)/shard_map/ppermute | solution.py:33
  54.7 1.9 %collective-permute-start.12 = (f32[8,128]{1,0:T(8,128)S(1)}, f32[8,128]{1,0:T(8,128)S(1)}, u32[]{:S(2)}, u32[]{:S(2)}) collective-permute-start(f32[8,128]{1,0:T(8,128)S(1)} %shard_map.71.u3), channel_id=1, source_target_pairs={{0,1},{1,0},{2,3},{3,2},{4,5},{5,4},{6,7},{7,6},{8,9},{9,8},{10,11... | collective-permute-start | bytes 12296 | tf_op jit(solution)/shard_map/ppermute | solution.py:33
  56.6 0.0 collective-permute-done.13
  56.6 1.1 collective-permute-done.12
  57.7 0.7 collective-permute-start.15
  58.4 6.3 %collective-permute-start.14 = (f32[3,8,128]{2,1,0:T(8,128)S(1)}, f32[3,8,128]{2,1,0:T(8,128)S(1)}, u32[]{:S(2)}, u32[]{:S(2)}) collective-permute-start(f32[3,8,128]{2,1,0:T(8,128)S(1)} %pad_maximum_fusion.3.own), channel_id=1, source_target_pairs={{0,8},{8,0},{16,24},{24,16},{32,40},{40,32},{48,56},{56,48},{64,72... | collective-permute-start | bytes 36872 | tf_op jit(solution)/shard_map/ppermute | solution.py:38
  64.7 0.0 collective-permute-done.15.odd
  64.8 1.1 collective-permute-done.14.even
  65.8 0.5 shard_map.72
  66.3 24.7 %all_to_all.10.parts = f32[32,1,128]{2,1,0:T(1,128)S(1)} all-to-all(f32[32,1,128]{2,1,0:T(1,128)S(1)} %shard_map.72), channel_id=1, replica_groups=mesh['y'=4,'z'=32,'x'=4,'core'=2] {'y','x','core'}, dimensions={0} | all-to-all | bytes 32768 | tf_op jit(solution)/shard_map/all_to_all | solution.py:236
  91.0 34.4 %all_to_all.11.parts = f32[32,1,128]{2,1,0:T(1,128)S(1)} all-to-all(f32[32,1,128]{2,1,0:T(1,128)S(1)} %shard_map.73), channel_id=1, replica_groups=mesh['y'=4,'z'=32,'x'=4,'core'=2] {'z'}, dimensions={0} | all-to-all | bytes 32768 | tf_op jit(solution)/shard_map/all_to_all | solution.py:244
  125.5 0.8 shard_map.74
  (6 shorter events, 0.1 us)
Async XLA Ops:
  0.6 17.6 %collective-permute-start.1 = (f32[8,128]{1,0:T(8,128)}, f32[8,128]{1,0:T(8,128)S(1)}, u32[]{:S(2)}, u32[]{:S(2)}) collective-permute-start(f32[8,128]{1,0:T(8,128)} %bitcast.48), channel_id=1, source_target_pairs={{1,2},{2,1},{3,4},{4,3},{5,6},{6,5},{9,10},{10,9},{11,12},{12,11},... | collective-permute-start | bytes 12296 | tf_op jit(solution)/shard_map/ppermute | solution.py:33
  5.1 13.2 %collective-permute-start = (f32[8,128]{1,0:T(8,128)}, f32[8,128]{1,0:T(8,128)S(1)}, u32[]{:S(2)}, u32[]{:S(2)}) collective-permute-start(f32[8,128]{1,0:T(8,128)} %bitcast.49), channel_id=1, source_target_pairs={{0,1},{1,0},{2,3},{3,2},{4,5},{5,4},{6,7},{7,6},{8,9},{9,8},{10,11... | collective-permute-start | bytes 12296 | tf_op jit(solution)/shard_map/ppermute | solution.py:33
  17.4 0.7 copy-start.2
  17.4 0.7 copy-start.3
  18.1 0.7 copy-start.1
  18.8 4.4 %collective-permute-start.3 = (f32[3,8,128]{2,1,0:T(8,128)S(1)}, f32[3,8,128]{2,1,0:T(8,128)S(1)}, u32[]{:S(2)}, u32[]{:S(2)}) collective-permute-start(f32[3,8,128]{2,1,0:T(8,128)S(1)} %pad_maximum_fusion.refs_1_), channel_id=1, source_target_pairs={{8,16},{16,8},{24,32},{32,24},{40,48},{48,40},{56,64},{64,56},{72,... | collective-permute-start | bytes 36872 | tf_op jit(solution)/shard_map/ppermute | solution.py:39
  19.5 4.4 %collective-permute-start.2 = (f32[3,8,128]{2,1,0:T(8,128)S(1)}, f32[3,8,128]{2,1,0:T(8,128)S(1)}, u32[]{:S(2)}, u32[]{:S(2)}) collective-permute-start(f32[3,8,128]{2,1,0:T(8,128)S(1)} %pad_maximum_fusion.refs_1_), channel_id=1, source_target_pairs={{0,8},{8,0},{16,24},{24,16},{32,40},{40,32},{48,56},{56,48},{64,72... | collective-permute-start | bytes 36872 | tf_op jit(solution)/shard_map/ppermute | solution.py:38
  21.5 2.4 %copy-start = (f32[1,1,8,128]{3,2,1,0:T(8,128)S(1)}, f32[1,1,8,128]{3,2,1,0:T(8,128)}, u32[]{:S(2)}) copy-start(f32[1,1,8,128]{3,2,1,0:T(8,128)} %param.9) | copy-start | bytes 12292
  24.3 4.9 %collective-permute-start.5 = (f32[8,128]{1,0:T(8,128)S(1)}, f32[8,128]{1,0:T(8,128)S(1)}, u32[]{:S(2)}, u32[]{:S(2)}) collective-permute-start(f32[8,128]{1,0:T(8,128)S(1)} %shard_map.69.u1), channel_id=1, source_target_pairs={{1,2},{2,1},{3,4},{4,3},{5,6},{6,5},{9,10},{10,9},{11,12},{12,11},... | collective-permute-start | bytes 12296 | tf_op jit(solution)/shard_map/ppermute | solution.py:33
  26.2 3.1 %collective-permute-start.4 = (f32[8,128]{1,0:T(8,128)S(1)}, f32[8,128]{1,0:T(8,128)S(1)}, u32[]{:S(2)}, u32[]{:S(2)}) collective-permute-start(f32[8,128]{1,0:T(8,128)S(1)} %shard_map.69.u1), channel_id=1, source_target_pairs={{0,1},{1,0},{2,3},{3,2},{4,5},{5,4},{6,7},{7,6},{8,9},{9,8},{10,11... | collective-permute-start | bytes 12296 | tf_op jit(solution)/shard_map/ppermute | solution.py:33
  29.3 4.6 %collective-permute-start.7 = (f32[3,8,128]{2,1,0:T(8,128)S(1)}, f32[3,8,128]{2,1,0:T(8,128)S(1)}, u32[]{:S(2)}, u32[]{:S(2)}) collective-permute-start(f32[3,8,128]{2,1,0:T(8,128)S(1)} %pad_maximum_fusion.1.refs_1_), channel_id=1, source_target_pairs={{8,16},{16,8},{24,32},{32,24},{40,48},{48,40},{56,64},{64,56},{72,... | collective-permute-start | bytes 36872 | tf_op jit(solution)/shard_map/ppermute | solution.py:39
  29.9 5.0 %collective-permute-start.6 = (f32[3,8,128]{2,1,0:T(8,128)S(1)}, f32[3,8,128]{2,1,0:T(8,128)S(1)}, u32[]{:S(2)}, u32[]{:S(2)}) collective-permute-start(f32[3,8,128]{2,1,0:T(8,128)S(1)} %pad_maximum_fusion.1.refs_1_), channel_id=1, source_target_pairs={{0,8},{8,0},{16,24},{24,16},{32,40},{40,32},{48,56},{56,48},{64,72... | collective-permute-start | bytes 36872 | tf_op jit(solution)/shard_map/ppermute | solution.py:38
  35.3 6.5 %collective-permute-start.9 = (f32[8,128]{1,0:T(8,128)S(1)}, f32[8,128]{1,0:T(8,128)S(1)}, u32[]{:S(2)}, u32[]{:S(2)}) collective-permute-start(f32[8,128]{1,0:T(8,128)S(1)} %shard_map.70.u2), channel_id=1, source_target_pairs={{1,2},{2,1},{3,4},{4,3},{5,6},{6,5},{9,10},{10,9},{11,12},{12,11},... | collective-permute-start | bytes 12296 | tf_op jit(solution)/shard_map/ppermute | solution.py:33
  39.8 3.1 %collective-permute-start.8 = (f32[8,128]{1,0:T(8,128)S(1)}, f32[8,128]{1,0:T(8,128)S(1)}, u32[]{:S(2)}, u32[]{:S(2)}) collective-permute-start(f32[8,128]{1,0:T(8,128)S(1)} %shard_map.70.u2), channel_id=1, source_target_pairs={{0,1},{1,0},{2,3},{3,2},{4,5},{5,4},{6,7},{7,6},{8,9},{9,8},{10,11... | collective-permute-start | bytes 12296 | tf_op jit(solution)/shard_map/ppermute | solution.py:33
  42.9 7.3 %collective-permute-start.11 = (f32[3,8,128]{2,1,0:T(8,128)S(1)}, f32[3,8,128]{2,1,0:T(8,128)S(1)}, u32[]{:S(2)}, u32[]{:S(2)}) collective-permute-start(f32[3,8,128]{2,1,0:T(8,128)S(1)} %pad_maximum_fusion.2.refs_1_), channel_id=1, source_target_pairs={{8,16},{16,8},{24,32},{32,24},{40,48},{48,40},{56,64},{64,56},{72,... | collective-permute-start | bytes 36872 | tf_op jit(solution)/shard_map/ppermute | solution.py:39
  43.5 7.7 %collective-permute-start.10 = (f32[3,8,128]{2,1,0:T(8,128)S(1)}, f32[3,8,128]{2,1,0:T(8,128)S(1)}, u32[]{:S(2)}, u32[]{:S(2)}) collective-permute-start(f32[3,8,128]{2,1,0:T(8,128)S(1)} %pad_maximum_fusion.2.refs_1_), channel_id=1, source_target_pairs={{0,8},{8,0},{16,24},{24,16},{32,40},{40,32},{48,56},{56,48},{64,72... | collective-permute-start | bytes 36872 | tf_op jit(solution)/shard_map/ppermute | solution.py:38
  51.6 5.0 %collective-permute-start.13 = (f32[8,128]{1,0:T(8,128)S(1)}, f32[8,128]{1,0:T(8,128)S(1)}, u32[]{:S(2)}, u32[]{:S(2)}) collective-permute-start(f32[8,128]{1,0:T(8,128)S(1)} %shard_map.71.u3), channel_id=1, source_target_pairs={{1,2},{2,1},{3,4},{4,3},{5,6},{6,5},{9,10},{10,9},{11,12},{12,11},... | collective-permute-start | bytes 12296 | tf_op jit(solution)/shard_map/ppermute | solution.py:33
  54.7 3.1 %collective-permute-start.12 = (f32[8,128]{1,0:T(8,128)S(1)}, f32[8,128]{1,0:T(8,128)S(1)}, u32[]{:S(2)}, u32[]{:S(2)}) collective-permute-start(f32[8,128]{1,0:T(8,128)S(1)} %shard_map.71.u3), channel_id=1, source_target_pairs={{0,1},{1,0},{2,3},{3,2},{4,5},{5,4},{6,7},{7,6},{8,9},{9,8},{10,11... | collective-permute-start | bytes 12296 | tf_op jit(solution)/shard_map/ppermute | solution.py:33
  57.7 7.0 %collective-permute-start.15 = (f32[3,8,128]{2,1,0:T(8,128)S(1)}, f32[3,8,128]{2,1,0:T(8,128)S(1)}, u32[]{:S(2)}, u32[]{:S(2)}) collective-permute-start(f32[3,8,128]{2,1,0:T(8,128)S(1)} %pad_maximum_fusion.3.own), channel_id=1, source_target_pairs={{8,16},{16,8},{24,32},{32,24},{40,48},{48,40},{56,64},{64,56},{72,... | collective-permute-start | bytes 36872 | tf_op jit(solution)/shard_map/ppermute | solution.py:39
  58.4 7.4 %collective-permute-start.14 = (f32[3,8,128]{2,1,0:T(8,128)S(1)}, f32[3,8,128]{2,1,0:T(8,128)S(1)}, u32[]{:S(2)}, u32[]{:S(2)}) collective-permute-start(f32[3,8,128]{2,1,0:T(8,128)S(1)} %pad_maximum_fusion.3.own), channel_id=1, source_target_pairs={{0,8},{8,0},{16,24},{24,16},{32,40},{40,32},{48,56},{56,48},{64,72... | collective-permute-start | bytes 36872 | tf_op jit(solution)/shard_map/ppermute | solution.py:38

commit v5 on v4

--- a/solution.py
+++ b/solution.py
@@ -12,7 +12,7 @@
 SLOTS = 4
 ROW = ("y", "z")
 COL = ("x", "core")
-PLANE = ("y", "x", "core")
+PLANE = ("core", "x", "y")
 SHIFT = 2.2
 PAIRS = [(i, j) for j in range(ITERS + 1) for i in range(j + 1)]
 F32 = jnp.float32
@@ -106,17 +106,19 @@
 
 def cholesky(gram, size):
     lower = [[None] * size for _ in range(size)]
+    inverse = []
     for j in range(size):
         pivot = gram[j][j]
         for k in range(j):
             pivot = pivot - lower[j][k] * lower[j][k]
         lower[j][j] = jnp.sqrt(pivot)
+        inverse.append(1.0 / lower[j][j])
         for i in range(j + 1, size):
             entry = gram[i][j]
             for k in range(j):
                 entry = entry - lower[i][k] * lower[j][k]
-            lower[i][j] = entry / lower[j][j]
-    return lower
+            lower[i][j] = entry * inverse[j]
+    return lower, inverse
 
 
 def finish_kernel(parts, u0, u1, u2, u3, solution_field, hessenberg):
@@ -129,7 +131,7 @@
     for at, (i, j) in enumerate(PAIRS):
         entry = jnp.sum(jnp.where(lane == at, total, 0.0), axis=1, keepdims=True)
         gram[i][j] = gram[j][i] = jnp.broadcast_to(entry, (NB, BS))
-    lower = cholesky(gram, size)
+    lower, inverse = cholesky(gram, size)
     h = [[None] * ITERS for _ in range(size)]
     for j in range(ITERS):
         for i in range(j + 2):
@@ -138,7 +140,7 @@
                 entry = entry + SHIFT * lower[j][i]
             for k in range(max(i - 1, 0), j):
                 entry = entry - h[i][k] * lower[j][k]
-            h[i][j] = entry / lower[j][j]
+            h[i][j] = entry * inverse[j]
     normal = [[None] * ITERS for _ in range(ITERS)]
     for i in range(ITERS):
         for j in range(i + 1):
@@ -146,25 +148,25 @@
             for k in range(1, j + 2):
                 entry = entry + h[k][i] * h[k][j]
             normal[i][j] = entry
-    factor = cholesky(normal, ITERS)
+    factor, scaled = cholesky(normal, ITERS)
     forward = []
     for i in range(ITERS):
         entry = lower[0][0] * h[0][i]
         for k in range(i):
             entry = entry - factor[i][k] * forward[k]
-        forward.append(entry / factor[i][i])
+        forward.append(entry * scaled[i])
     y = [None] * ITERS
     for i in reversed(range(ITERS)):
         entry = forward[i]
         for k in range(i + 1, ITERS):
             entry = entry - factor[k][i] * y[k]
-        y[i] = entry / factor[i][i]
+        y[i] = entry * scaled[i]
     weights = [None] * ITERS
     for i in reversed(range(ITERS)):
         entry = y[i]
         for k in range(i + 1, ITERS):
             entry = entry - lower[k][i] * weights[k]
-        weights[i] = entry / lower[i][i]
+        weights[i] = entry * inverse[i]
     solution_field[...] = (weights[0] * u0[...] + weights[1] * u1[...]) + (
         weights[2] * u2[...] + weights[3] * u3[...]
     )

time: 127 us -> 127 us (level)
  no operation moved by 1% of the time
where the time goes in v5:
time: 127 us; the launch traced here: 126 us
  blocking collectives  59 us (46%)
  starting transfers between devices  53.4 us (42%)
  waiting for transfers between devices  7.46 us (6%)
  Pallas kernels  4.15 us (3%)
    all_to_all x1, blocking collectives, on_device(): parts = lax.all_to_all(parts, 'z', split_axis=0, concat_axis=0, tiled=True)  34.4 us
    all_to_all x1, blocking collectives, on_device(): lax.all_to_all(parts, PLANE, split_axis=0, concat_axis=0, tiled=True)  24.6 us
    ppermute x4, starting transfers between devices, exchange(): lax.ppermute(beside, ROW, even)  18.8 us
    ppermute x4, starting transfers between devices, exchange(): lax.ppermute(field, COL, even)  18 us
    ppermute x4, starting transfers between devices, exchange(): lax.ppermute(field, COL, odd)  14 us
    ppermute x4, waiting for transfers between devices, exchange(): lax.ppermute(beside, ROW, even)  3.89 us
    ppermute x4, starting transfers between devices, exchange(): lax.ppermute(beside, ROW, odd)  2.6 us
  transfers between devices with their start and end apart: 16, of which 9 were waited for; matrix products, arithmetic and copies ran while one was open for 0% of the time, Pallas kernels for 1%

profile of v5, /device:TPU:1, one launch (start us, length us, event | category | flops | bytes accessed | tf_op | source)
XLA Modules:
  0.0 126.1 jit_solution(10733706038437842026)
XLA Ops:
  0.6 4.5 %collective-permute-start.1 = (f32[8,128]{1,0:T(8,128)}, f32[8,128]{1,0:T(8,128)S(1)}, u32[]{:S(2)}, u32[]{:S(2)}) collective-permute-start(f32[8,128]{1,0:T(8,128)} %bitcast.48), channel_id=1, source_target_pairs={{1,2},{2,1},{3,4},{4,3},{5,6},{6,5},{9,10},{10,9},{11,12},{12,11},... | collective-permute-start | bytes 12296 | tf_op jit(solution)/shard_map/ppermute | solution.py:33
  5.1 12.2 %collective-permute-start = (f32[8,128]{1,0:T(8,128)}, f32[8,128]{1,0:T(8,128)S(1)}, u32[]{:S(2)}, u32[]{:S(2)}) collective-permute-start(f32[8,128]{1,0:T(8,128)} %bitcast.49), channel_id=1, source_target_pairs={{0,1},{1,0},{2,3},{3,2},{4,5},{5,4},{6,7},{7,6},{8,9},{9,8},{10,11... | collective-permute-start | bytes 12296 | tf_op jit(solution)/shard_map/ppermute | solution.py:33
  17.4 0.0 copy-start.2
  17.4 0.0 copy-start.3
  17.4 0.7 copy-done.2
  18.1 0.0 copy-done.3
  18.1 0.0 copy-start.1
  18.1 0.1 eq.41
  18.2 0.0 collective-permute-done.1
  18.2 0.2 collective-permute-done
  18.4 0.4 copy-done.1
  18.8 0.7 collective-permute-start.3
  19.5 1.9 %collective-permute-start.2 = (f32[3,8,128]{2,1,0:T(8,128)S(1)}, f32[3,8,128]{2,1,0:T(8,128)S(1)}, u32[]{:S(2)}, u32[]{:S(2)}) collective-permute-start(f32[3,8,128]{2,1,0:T(8,128)S(1)} %pad_maximum_fusion.refs_1_), channel_id=1, source_target_pairs={{0,8},{8,0},{16,24},{24,16},{32,40},{40,32},{48,56},{56,48},{64,72... | collective-permute-start | bytes 36872 | tf_op jit(solution)/shard_map/ppermute | solution.py:38
  21.4 0.1 fusion.refs_0_.pick
  21.5 0.0 copy-start
  21.5 1.7 %shard_map.68.refs_4_.values = bf16[32,128,128]{2,1,0:T(8,128)(2,1)S(1)} custom-call(bf16[32,128,128]{2,1,0:T(8,128)(2,1)} %bitcast.54), custom_call_target="tpu_custom_call" | custom-call | tf_op jit(solution)/shard_map/pallas_call | solution.py:203
  23.2 0.0 collective-permute-done.3.refs_3_
  23.2 0.7 collective-permute-done.2.refs_2_
  23.9 0.0 copy-done
  23.9 0.4 shard_map.69.u1
  24.3 1.9 %collective-permute-start.5 = (f32[8,128]{1,0:T(8,128)S(1)}, f32[8,128]{1,0:T(8,128)S(1)}, u32[]{:S(2)}, u32[]{:S(2)}) collective-permute-start(f32[8,128]{1,0:T(8,128)S(1)} %shard_map.69.u1), channel_id=1, source_target_pairs={{1,2},{2,1},{3,4},{4,3},{5,6},{6,5},{9,10},{10,9},{11,12},{12,11},... | collective-permute-start | bytes 12296 | tf_op jit(solution)/shard_map/ppermute | solution.py:33
  26.2 1.9 %collective-permute-start.4 = (f32[8,128]{1,0:T(8,128)S(1)}, f32[8,128]{1,0:T(8,128)S(1)}, u32[]{:S(2)}, u32[]{:S(2)}) collective-permute-start(f32[8,128]{1,0:T(8,128)S(1)} %shard_map.69.u1), channel_id=1, source_target_pairs={{0,1},{1,0},{2,3},{3,2},{4,5},{5,4},{6,7},{7,6},{8,9},{9,8},{10,11... | collective-permute-start | bytes 12296 | tf_op jit(solution)/shard_map/ppermute | solution.py:33
  28.1 1.1 collective-permute-done.5
  29.2 0.1 collective-permute-done.4
  29.3 0.7 collective-permute-start.7
  29.9 3.9 %collective-permute-start.6 = (f32[3,8,128]{2,1,0:T(8,128)S(1)}, f32[3,8,128]{2,1,0:T(8,128)S(1)}, u32[]{:S(2)}, u32[]{:S(2)}) collective-permute-start(f32[3,8,128]{2,1,0:T(8,128)S(1)} %pad_maximum_fusion.1.refs_1_), channel_id=1, source_target_pairs={{0,8},{8,0},{16,24},{24,16},{32,40},{40,32},{48,56},{56,48},{64,72... | collective-permute-start | bytes 36872 | tf_op jit(solution)/shard_map/ppermute | solution.py:38
  33.8 0.0 collective-permute-done.7.refs_3_
  33.9 1.1 collective-permute-done.6.refs_2_
  34.9 0.4 shard_map.70.u2
  35.3 4.5 %collective-permute-start.9 = (f32[8,128]{1,0:T(8,128)S(1)}, f32[8,128]{1,0:T(8,128)S(1)}, u32[]{:S(2)}, u32[]{:S(2)}) collective-permute-start(f32[8,128]{1,0:T(8,128)S(1)} %shard_map.70.u2), channel_id=1, source_target_pairs={{1,2},{2,1},{3,4},{4,3},{5,6},{6,5},{9,10},{10,9},{11,12},{12,11},... | collective-permute-start | bytes 12296 | tf_op jit(solution)/shard_map/ppermute | solution.py:33
  39.8 1.9 %collective-permute-start.8 = (f32[8,128]{1,0:T(8,128)S(1)}, f32[8,128]{1,0:T(8,128)S(1)}, u32[]{:S(2)}, u32[]{:S(2)}) collective-permute-start(f32[8,128]{1,0:T(8,128)S(1)} %shard_map.70.u2), channel_id=1, source_target_pairs={{0,1},{1,0},{2,3},{3,2},{4,5},{5,4},{6,7},{7,6},{8,9},{9,8},{10,11... | collective-permute-start | bytes 12296 | tf_op jit(solution)/shard_map/ppermute | solution.py:33
  41.7 0.0 collective-permute-done.9
  41.7 1.1 collective-permute-done.8
  42.9 0.7 collective-permute-start.11
  43.5 6.6 %collective-permute-start.10 = (f32[3,8,128]{2,1,0:T(8,128)S(1)}, f32[3,8,128]{2,1,0:T(8,128)S(1)}, u32[]{:S(2)}, u32[]{:S(2)}) collective-permute-start(f32[3,8,128]{2,1,0:T(8,128)S(1)} %pad_maximum_fusion.2.refs_1_), channel_id=1, source_target_pairs={{0,8},{8,0},{16,24},{24,16},{32,40},{40,32},{48,56},{56,48},{64,72... | collective-permute-start | bytes 36872 | tf_op jit(solution)/shard_map/ppermute | solution.py:38
  50.2 0.0 collective-permute-done.11.refs_3_
  50.2 1.1 collective-permute-done.10.refs_2_
  51.2 0.4 shard_map.71.u3
  51.6 3.1 %collective-permute-start.13 = (f32[8,128]{1,0:T(8,128)S(1)}, f32[8,128]{1,0:T(8,128)S(1)}, u32[]{:S(2)}, u32[]{:S(2)}) collective-permute-start(f32[8,128]{1,0:T(8,128)S(1)} %shard_map.71.u3), channel_id=1, source_target_pairs={{1,2},{2,1},{3,4},{4,3},{5,6},{6,5},{9,10},{10,9},{11,12},{12,11},... | collective-permute-start | bytes 12296 | tf_op jit(solution)/shard_map/ppermute | solution.py:33
  54.7 1.9 %collective-permute-start.12 = (f32[8,128]{1,0:T(8,128)S(1)}, f32[8,128]{1,0:T(8,128)S(1)}, u32[]{:S(2)}, u32[]{:S(2)}) collective-permute-start(f32[8,128]{1,0:T(8,128)S(1)} %shard_map.71.u3), channel_id=1, source_target_pairs={{0,1},{1,0},{2,3},{3,2},{4,5},{5,4},{6,7},{7,6},{8,9},{9,8},{10,11... | collective-permute-start | bytes 12296 | tf_op jit(solution)/shard_map/ppermute | solution.py:33
  56.6 0.0 collective-permute-done.13
  56.6 1.1 collective-permute-done.12
  57.7 0.7 collective-permute-start.15
  58.4 6.3 %collective-permute-start.14 = (f32[3,8,128]{2,1,0:T(8,128)S(1)}, f32[3,8,128]{2,1,0:T(8,128)S(1)}, u32[]{:S(2)}, u32[]{:S(2)}) collective-permute-start(f32[3,8,128]{2,1,0:T(8,128)S(1)} %pad_maximum_fusion.3.own), channel_id=1, source_target_pairs={{0,8},{8,0},{16,24},{24,16},{32,40},{40,32},{48,56},{56,48},{64,72... | collective-permute-start | bytes 36872 | tf_op jit(solution)/shard_map/ppermute | solution.py:38
  64.7 0.0 collective-permute-done.15.odd
  64.8 1.1 collective-permute-done.14.even
  65.8 0.5 shard_map.72
  66.3 24.6 %all_to_all.10.parts = f32[32,1,128]{2,1,0:T(1,128)S(1)} all-to-all(f32[32,1,128]{2,1,0:T(1,128)S(1)} %shard_map.72), channel_id=1, replica_groups=mesh['y'=4,'z'=32,'x'=4,'core'=2] {'core','x','y'}, dimensions={0} | all-to-all | bytes 32768 | tf_op jit(solution)/shard_map/all_to_all | solution.py:238
  91.0 34.4 %all_to_all.11.parts = f32[32,1,128]{2,1,0:T(1,128)S(1)} all-to-all(f32[32,1,128]{2,1,0:T(1,128)S(1)} %shard_map.73), channel_id=1, replica_groups=mesh['y'=4,'z'=32,'x'=4,'core'=2] {'z'}, dimensions={0} | all-to-all | bytes 32768 | tf_op jit(solution)/shard_map/all_to_all | solution.py:246
  125.3 0.8 shard_map.74
  (6 shorter events, 0.1 us)
Async XLA Ops:
  0.6 17.6 %collective-permute-start.1 = (f32[8,128]{1,0:T(8,128)}, f32[8,128]{1,0:T(8,128)S(1)}, u32[]{:S(2)}, u32[]{:S(2)}) collective-permute-start(f32[8,128]{1,0:T(8,128)} %bitcast.48), channel_id=1, source_target_pairs={{1,2},{2,1},{3,4},{4,3},{5,6},{6,5},{9,10},{10,9},{11,12},{12,11},... | collective-permute-start | bytes 12296 | tf_op jit(solution)/shard_map/ppermute | solution.py:33
  5.1 13.2 %collective-permute-start = (f32[8,128]{1,0:T(8,128)}, f32[8,128]{1,0:T(8,128)S(1)}, u32[]{:S(2)}, u32[]{:S(2)}) collective-permute-start(f32[8,128]{1,0:T(8,128)} %bitcast.49), channel_id=1, source_target_pairs={{0,1},{1,0},{2,3},{3,2},{4,5},{5,4},{6,7},{7,6},{8,9},{9,8},{10,11... | collective-permute-start | bytes 12296 | tf_op jit(solution)/shard_map/ppermute | solution.py:33
  17.4 0.7 copy-start.2
  17.4 0.7 copy-start.3
  18.1 0.7 copy-start.1
  18.8 4.4 %collective-permute-start.3 = (f32[3,8,128]{2,1,0:T(8,128)S(1)}, f32[3,8,128]{2,1,0:T(8,128)S(1)}, u32[]{:S(2)}, u32[]{:S(2)}) collective-permute-start(f32[3,8,128]{2,1,0:T(8,128)S(1)} %pad_maximum_fusion.refs_1_), channel_id=1, source_target_pairs={{8,16},{16,8},{24,32},{32,24},{40,48},{48,40},{56,64},{64,56},{72,... | collective-permute-start | bytes 36872 | tf_op jit(solution)/shard_map/ppermute | solution.py:39
  19.5 4.4 %collective-permute-start.2 = (f32[3,8,128]{2,1,0:T(8,128)S(1)}, f32[3,8,128]{2,1,0:T(8,128)S(1)}, u32[]{:S(2)}, u32[]{:S(2)}) collective-permute-start(f32[3,8,128]{2,1,0:T(8,128)S(1)} %pad_maximum_fusion.refs_1_), channel_id=1, source_target_pairs={{0,8},{8,0},{16,24},{24,16},{32,40},{40,32},{48,56},{56,48},{64,72... | collective-permute-start | bytes 36872 | tf_op jit(solution)/shard_map/ppermute | solution.py:38
  21.5 2.4 %copy-start = (f32[1,1,8,128]{3,2,1,0:T(8,128)S(1)}, f32[1,1,8,128]{3,2,1,0:T(8,128)}, u32[]{:S(2)}) copy-start(f32[1,1,8,128]{3,2,1,0:T(8,128)} %param.9) | copy-start | bytes 12292
  24.3 4.9 %collective-permute-start.5 = (f32[8,128]{1,0:T(8,128)S(1)}, f32[8,128]{1,0:T(8,128)S(1)}, u32[]{:S(2)}, u32[]{:S(2)}) collective-permute-start(f32[8,128]{1,0:T(8,128)S(1)} %shard_map.69.u1), channel_id=1, source_target_pairs={{1,2},{2,1},{3,4},{4,3},{5,6},{6,5},{9,10},{10,9},{11,12},{12,11},... | collective-permute-start | bytes 12296 | tf_op jit(solution)/shard_map/ppermute | solution.py:33
  26.2 3.1 %collective-permute-start.4 = (f32[8,128]{1,0:T(8,128)S(1)}, f32[8,128]{1,0:T(8,128)S(1)}, u32[]{:S(2)}, u32[]{:S(2)}) collective-permute-start(f32[8,128]{1,0:T(8,128)S(1)} %shard_map.69.u1), channel_id=1, source_target_pairs={{0,1},{1,0},{2,3},{3,2},{4,5},{5,4},{6,7},{7,6},{8,9},{9,8},{10,11... | collective-permute-start | bytes 12296 | tf_op jit(solution)/shard_map/ppermute | solution.py:33
  29.3 4.6 %collective-permute-start.7 = (f32[3,8,128]{2,1,0:T(8,128)S(1)}, f32[3,8,128]{2,1,0:T(8,128)S(1)}, u32[]{:S(2)}, u32[]{:S(2)}) collective-permute-start(f32[3,8,128]{2,1,0:T(8,128)S(1)} %pad_maximum_fusion.1.refs_1_), channel_id=1, source_target_pairs={{8,16},{16,8},{24,32},{32,24},{40,48},{48,40},{56,64},{64,56},{72,... | collective-permute-start | bytes 36872 | tf_op jit(solution)/shard_map/ppermute | solution.py:39
  29.9 5.0 %collective-permute-start.6 = (f32[3,8,128]{2,1,0:T(8,128)S(1)}, f32[3,8,128]{2,1,0:T(8,128)S(1)}, u32[]{:S(2)}, u32[]{:S(2)}) collective-permute-start(f32[3,8,128]{2,1,0:T(8,128)S(1)} %pad_maximum_fusion.1.refs_1_), channel_id=1, source_target_pairs={{0,8},{8,0},{16,24},{24,16},{32,40},{40,32},{48,56},{56,48},{64,72... | collective-permute-start | bytes 36872 | tf_op jit(solution)/shard_map/ppermute | solution.py:38
  35.3 6.5 %collective-permute-start.9 = (f32[8,128]{1,0:T(8,128)S(1)}, f32[8,128]{1,0:T(8,128)S(1)}, u32[]{:S(2)}, u32[]{:S(2)}) collective-permute-start(f32[8,128]{1,0:T(8,128)S(1)} %shard_map.70.u2), channel_id=1, source_target_pairs={{1,2},{2,1},{3,4},{4,3},{5,6},{6,5},{9,10},{10,9},{11,12},{12,11},... | collective-permute-start | bytes 12296 | tf_op jit(solution)/shard_map/ppermute | solution.py:33
  39.8 3.1 %collective-permute-start.8 = (f32[8,128]{1,0:T(8,128)S(1)}, f32[8,128]{1,0:T(8,128)S(1)}, u32[]{:S(2)}, u32[]{:S(2)}) collective-permute-start(f32[8,128]{1,0:T(8,128)S(1)} %shard_map.70.u2), channel_id=1, source_target_pairs={{0,1},{1,0},{2,3},{3,2},{4,5},{5,4},{6,7},{7,6},{8,9},{9,8},{10,11... | collective-permute-start | bytes 12296 | tf_op jit(solution)/shard_map/ppermute | solution.py:33
  42.9 7.3 %collective-permute-start.11 = (f32[3,8,128]{2,1,0:T(8,128)S(1)}, f32[3,8,128]{2,1,0:T(8,128)S(1)}, u32[]{:S(2)}, u32[]{:S(2)}) collective-permute-start(f32[3,8,128]{2,1,0:T(8,128)S(1)} %pad_maximum_fusion.2.refs_1_), channel_id=1, source_target_pairs={{8,16},{16,8},{24,32},{32,24},{40,48},{48,40},{56,64},{64,56},{72,... | collective-permute-start | bytes 36872 | tf_op jit(solution)/shard_map/ppermute | solution.py:39
  43.5 7.7 %collective-permute-start.10 = (f32[3,8,128]{2,1,0:T(8,128)S(1)}, f32[3,8,128]{2,1,0:T(8,128)S(1)}, u32[]{:S(2)}, u32[]{:S(2)}) collective-permute-start(f32[3,8,128]{2,1,0:T(8,128)S(1)} %pad_maximum_fusion.2.refs_1_), channel_id=1, source_target_pairs={{0,8},{8,0},{16,24},{24,16},{32,40},{40,32},{48,56},{56,48},{64,72... | collective-permute-start | bytes 36872 | tf_op jit(solution)/shard_map/ppermute | solution.py:38
  51.6 5.0 %collective-permute-start.13 = (f32[8,128]{1,0:T(8,128)S(1)}, f32[8,128]{1,0:T(8,128)S(1)}, u32[]{:S(2)}, u32[]{:S(2)}) collective-permute-start(f32[8,128]{1,0:T(8,128)S(1)} %shard_map.71.u3), channel_id=1, source_target_pairs={{1,2},{2,1},{3,4},{4,3},{5,6},{6,5},{9,10},{10,9},{11,12},{12,11},... | collective-permute-start | bytes 12296 | tf_op jit(solution)/shard_map/ppermute | solution.py:33
  54.7 3.1 %collective-permute-start.12 = (f32[8,128]{1,0:T(8,128)S(1)}, f32[8,128]{1,0:T(8,128)S(1)}, u32[]{:S(2)}, u32[]{:S(2)}) collective-permute-start(f32[8,128]{1,0:T(8,128)S(1)} %shard_map.71.u3), channel_id=1, source_target_pairs={{0,1},{1,0},{2,3},{3,2},{4,5},{5,4},{6,7},{7,6},{8,9},{9,8},{10,11... | collective-permute-start | bytes 12296 | tf_op jit(solution)/shard_map/ppermute | solution.py:33
  57.7 7.0 %collective-permute-start.15 = (f32[3,8,128]{2,1,0:T(8,128)S(1)}, f32[3,8,128]{2,1,0:T(8,128)S(1)}, u32[]{:S(2)}, u32[]{:S(2)}) collective-permute-start(f32[3,8,128]{2,1,0:T(8,128)S(1)} %pad_maximum_fusion.3.own), channel_id=1, source_target_pairs={{8,16},{16,8},{24,32},{32,24},{40,48},{48,40},{56,64},{64,56},{72,... | collective-permute-start | bytes 36872 | tf_op jit(solution)/shard_map/ppermute | solution.py:39
  58.4 7.4 %collective-permute-start.14 = (f32[3,8,128]{2,1,0:T(8,128)S(1)}, f32[3,8,128]{2,1,0:T(8,128)S(1)}, u32[]{:S(2)}, u32[]{:S(2)}) collective-permute-start(f32[3,8,128]{2,1,0:T(8,128)S(1)} %pad_maximum_fusion.3.own), channel_id=1, source_target_pairs={{0,8},{8,0},{16,24},{24,16},{32,40},{40,32},{48,56},{56,48},{64,72... | collective-permute-start | bytes 36872 | tf_op jit(solution)/shard_map/ppermute | solution.py:38
